TPU v7x, 256 devices: a whole 4x4x8 slice. The times are simulated.
256 devices in a mesh: lat: 8 (over y, x_hi), lon: 32 (over z, x_lo, core).
Axes of the slice: x: 4 (x_hi: 2, x_lo: 2; x = x_hi * 2 + x_lo), y: 4, z: 8, core: 2. Of those that a mesh axis runs over, the one named last changes fastest.
Arguments:
- inputs: bfloat16 [64, 512, 1024], P('lat', 'lon'), may hold values from -24 to 24
- input_weight: bfloat16 [2, 1024, 1536], replicated, may hold values from -0.1875 to 0.1875
- output_weight: bfloat16 [2, 512, 1024], replicated, may hold values from -0.25 to 0.25
- norm_gain: float32 [2, 1024], replicated, may hold values from 0.1 to 1.9
- position_bias: float32 [2, 8, 49], replicated, may hold values from -6 to 260
- cotangent: bfloat16 [64, 512, 1024], P('lat', 'lon'), may hold values from -6 to 6
Outputs:
- output: bfloat16 [64, 512, 1024], P('lat', 'lon')
- input_grad: bfloat16 [64, 512, 1024], P('lat', 'lon')
- input_weight_grad: float32 [2, 1024, 1536], P(None, 'lon')
- output_weight_grad: float32 [2, 512, 1024], P(None, 'lon')
- norm_gain_grad: float32 [2, 1024], replicated
- position_bias_grad: float32 [2, 8, 49], replicated
All inputs are finite; a program needn't handle non-finite values.
Results may differ from a plain program's by a relative error of at most 0.04.
Values may be sent and summed in bfloat16 or wider, within the bound.
A program may use at most 128 MiB of HBM per device.

v0:
```python
import jax
import jax.numpy as jnp
from jax import lax
from jax.sharding import PartitionSpec as P

HEADS = 8
HEAD_DIM = 64
WIN = 7
LAYERS = 2


eps = 1e-05


def extended(block, sides, width):
    for axis, dim in sides:
        count = lax.axis_size(axis)
        forward = [(i, i + 1) for i in range(count - 1)]
        forward.append((count - 1, 0))
        backward = [(target, source) for source, target in forward]
        low = lax.ppermute(
            lax.slice_in_dim(block, block.shape[dim] - width, None, axis=dim), axis, forward
        )
        high = lax.ppermute(lax.slice_in_dim(block, 0, width, axis=dim), axis, backward)
        block = jnp.concatenate([low, block, high], axis=dim)
    return block


def layer_norm(wide_input, gain):
    row_mean = jnp.mean(wide_input, axis=-1, keepdims=True)
    centred = wide_input - row_mean
    variance = jnp.mean(centred * centred, axis=-1, keepdims=True)
    return centred * lax.rsqrt(variance + eps) * gain


def cell_coords(rows, cols, shift):
    row_ids = jnp.arange(rows, dtype=jnp.int32)[:, None] + jnp.zeros((1, cols), jnp.int32) + shift
    col_ids = jnp.arange(cols, dtype=jnp.int32)[None, :] + jnp.zeros((rows, 1), jnp.int32) + shift
    return (row_ids.reshape(-1), col_ids.reshape(-1))


def window_table(query_rows, query_cols, query_shift, key_rows, key_cols, key_shift):
    radius = WIN // 2
    query_i, query_j = cell_coords(query_rows, query_cols, query_shift)
    key_i, key_j = cell_coords(key_rows, key_cols, key_shift)
    offsets = jnp.arange(WIN * WIN, dtype=jnp.int32)
    step_lat = offsets // WIN - radius
    step_lon = offsets % WIN - radius
    match_lat = key_i[None, None, :] - query_i[:, None, None] == step_lat[None, :, None]
    match_lon = key_j[None, None, :] - query_j[:, None, None] == step_lon[None, :, None]
    return match_lat & match_lon


def attend(queries, keys_wide, values_wide, bias, allowed, table_full):
    tile_rows, tile_cols = (queries.shape[0], queries.shape[1])
    score_scale = HEAD_DIM ** (-0.5)
    cells = tile_rows * tile_cols
    query_heads = queries.reshape(cells, HEADS, HEAD_DIM)
    key_heads = keys_wide.reshape(-1, HEADS, HEAD_DIM)
    value_heads = values_wide.reshape(-1, HEADS, HEAD_DIM)
    raw = jnp.einsum("qhd,khd->hqk", query_heads, key_heads, preferred_element_type=jnp.float32)
    bias_dense = jnp.einsum("ho,qok->hqk", bias, table_full, precision=lax.Precision.HIGHEST)
    scores = raw * score_scale + bias_dense
    masked = jnp.where(allowed[None], scores, -jnp.inf)
    row_max = jnp.max(masked, axis=-1, keepdims=True)
    weights_exp = jnp.exp(masked - row_max)
    attention = weights_exp / jnp.sum(weights_exp, axis=-1, keepdims=True)
    probs_low = attention.astype(jnp.bfloat16)
    mixed = jnp.einsum("hqk,khd->qhd", probs_low, value_heads, preferred_element_type=jnp.float32)
    return (
        attention,
        probs_low,
        mixed.reshape(tile_rows, tile_cols, HEADS * HEAD_DIM).astype(jnp.bfloat16),
    )


def pull_back(received, back_table):
    inner_width = HEADS * HEAD_DIM
    spread = HEADS * WIN * WIN
    flat = received.reshape(-1, received.shape[-1])
    query_heads = flat[:, :inner_width].reshape(-1, HEADS, HEAD_DIM)
    grad_heads = flat[:, inner_width : 2 * inner_width].reshape(-1, HEADS, HEAD_DIM)
    prob_piece = flat[:, 2 * inner_width : 2 * inner_width + spread].reshape(-1, HEADS, WIN * WIN)
    score_piece = flat[:, 2 * inner_width + spread :].reshape(-1, HEADS, WIN * WIN)
    score_dense = jnp.einsum(
        "qho,qok->hqk", score_piece, back_table, preferred_element_type=jnp.float32
    ).astype(jnp.bfloat16)
    prob_dense = jnp.einsum(
        "qho,qok->hqk", prob_piece, back_table, preferred_element_type=jnp.float32
    ).astype(jnp.bfloat16)
    grad_keys = jnp.einsum(
        "hqk,qhd->khd", score_dense, query_heads, preferred_element_type=jnp.float32
    )
    grad_values = jnp.einsum(
        "hqk,qhd->khd", prob_dense, grad_heads, preferred_element_type=jnp.float32
    )
    return (grad_keys * HEAD_DIM ** (-0.5), grad_values)


def shards(inputs, input_weight, output_weight, norm_gain, position_bias, cotangent):
    radius = WIN // 2
    inner_width = HEADS * HEAD_DIM
    score_scale = HEAD_DIM ** (-0.5)
    tile_rows, tile_cols = (inputs.shape[0], inputs.shape[1])
    cells = tile_rows * tile_cols
    wide_rows = tile_rows + 2 * radius
    wide_cols = tile_cols + 2 * radius
    first_row = lax.axis_index("lat") * tile_rows - radius
    global_rows = first_row + jnp.arange(wide_rows, dtype=jnp.int32)
    valid_rows = (global_rows >= 0) & (global_rows < tile_rows * lax.axis_size("lat"))
    row_keep = valid_rows.astype(jnp.bfloat16)[:, None, None]
    key_valid = (valid_rows[:, None] & jnp.ones((1, wide_cols), jnp.bool_)).reshape(-1)
    forward_table = window_table(tile_rows, tile_cols, radius, wide_rows, wide_cols, 0)
    table_low = forward_table.astype(jnp.bfloat16)
    table_full = forward_table.astype(jnp.float32)
    allowed = jnp.any(forward_table, axis=1) & key_valid[None, :]
    back_table = window_table(wide_rows, wide_cols, 0, tile_rows, tile_cols, radius).astype(
        jnp.bfloat16
    )
    stream = inputs
    stored = []
    for layer_idx in range(LAYERS):
        wide_input = stream.astype(jnp.float32)
        normed_wide, pullback = jax.vjp(layer_norm, wide_input, norm_gain[layer_idx])
        normed = normed_wide.astype(jnp.bfloat16)
        packed = jnp.einsum(
            "abd,de->abe", normed, input_weight[layer_idx], preferred_element_type=jnp.float32
        ).astype(jnp.bfloat16)
        queries = packed[..., :inner_width]
        key_value = packed[..., inner_width:]
        pair_wide = extended(key_value, (("lat", 0), ("lon", 1)), radius)
        keys_wide = pair_wide[..., :inner_width]
        values_wide = pair_wide[..., inner_width:]
        attention, probs_low, mixed = attend(
            queries, keys_wide, values_wide, position_bias[layer_idx], allowed, table_full
        )
        branch = jnp.einsum(
            "abi,id->abd", mixed, output_weight[layer_idx], preferred_element_type=jnp.float32
        )
        stored.append(
            (pullback, normed, queries, keys_wide, values_wide, attention, probs_low, mixed)
        )
        stream = (wide_input + branch).astype(jnp.bfloat16)
    upstream = cotangent
    packed_terms = [None] * LAYERS
    output_terms = [None] * LAYERS
    gain_terms = [None] * LAYERS
    bias_terms = [None] * LAYERS
    for layer_idx in reversed(range(LAYERS)):
        pullback, normed, queries, keys_wide, values_wide, attention, probs_low, mixed = stored[
            layer_idx
        ]
        output_term = jnp.einsum("abi,abd->id", mixed, upstream, preferred_element_type=jnp.float32)
        grad_mixed = jnp.einsum(
            "abd,id->abi", upstream, output_weight[layer_idx], preferred_element_type=jnp.float32
        ).astype(jnp.bfloat16)
        grad_heads = grad_mixed.reshape(cells, HEADS, HEAD_DIM)
        key_heads = keys_wide.reshape(-1, HEADS, HEAD_DIM)
        value_heads = values_wide.reshape(-1, HEADS, HEAD_DIM)
        grad_probs = jnp.einsum(
            "qhd,khd->hqk", grad_heads, value_heads, preferred_element_type=jnp.float32
        )
        row_delta = jnp.sum(attention * grad_probs, axis=-1, keepdims=True)
        grad_scores = attention * (grad_probs - row_delta)
        bias_terms[layer_idx] = jnp.einsum(
            "hqk,qok->ho", grad_scores, table_full, precision=lax.Precision.HIGHEST
        )
        scores_low = grad_scores.astype(jnp.bfloat16)
        grad_query = jnp.einsum(
            "hqk,khd->qhd", scores_low, key_heads, preferred_element_type=jnp.float32
        )
        probs_offset = jnp.einsum(
            "hqk,qok->qho", probs_low, table_low, preferred_element_type=jnp.float32
        ).astype(jnp.bfloat16)
        scores_offset = jnp.einsum(
            "hqk,qok->qho", scores_low, table_low, preferred_element_type=jnp.float32
        ).astype(jnp.bfloat16)
        outgoing = jnp.concatenate(
            [
                queries,
                grad_mixed,
                probs_offset.reshape(tile_rows, tile_cols, HEADS * WIN * WIN),
                scores_offset.reshape(tile_rows, tile_cols, HEADS * WIN * WIN),
            ],
            axis=-1,
        )
        received = extended(outgoing, (("lat", 0), ("lon", 1)), radius) * row_keep
        grad_keys, grad_values = pull_back(received, back_table)
        grad_packed = jnp.concatenate(
            [
                (grad_query * score_scale).reshape(tile_rows, tile_cols, inner_width),
                grad_keys.reshape(tile_rows, tile_cols, inner_width),
                grad_values.reshape(tile_rows, tile_cols, inner_width),
            ],
            axis=-1,
        ).astype(jnp.bfloat16)
        packed_term = jnp.einsum(
            "abd,abe->de", normed, grad_packed, preferred_element_type=jnp.float32
        )
        grad_normed = jnp.einsum(
            "abe,de->abd", grad_packed, input_weight[layer_idx], preferred_element_type=jnp.float32
        )
        grad_wide, gain_term = pullback(grad_normed)
        gain_terms[layer_idx] = gain_term
        upstream = (upstream.astype(jnp.float32) + grad_wide).astype(jnp.bfloat16)
        packed_terms[layer_idx] = packed_term
        output_terms[layer_idx] = output_term
    lon_share = (
        lax.psum_scatter(
            jnp.stack(packed_terms).astype(jnp.bfloat16), "lon", scatter_dimension=1, tiled=True
        ).astype(jnp.float32),
        lax.psum_scatter(
            jnp.stack(output_terms).astype(jnp.bfloat16), "lon", scatter_dimension=1, tiled=True
        ).astype(jnp.float32),
    )
    packed_grad, output_grad = (
        lax.psum(lon_share[0].astype(jnp.bfloat16), "lat").astype(jnp.float32),
        lax.psum(lon_share[1].astype(jnp.bfloat16), "lat").astype(jnp.float32),
    )
    gain_grad, bias_grad = lax.psum((jnp.stack(gain_terms), jnp.stack(bias_terms)), ("lat", "lon"))
    return (stream, upstream, packed_grad, output_grad, gain_grad, bias_grad)


def solution(mesh):
    return jax.shard_map(
        shards,
        mesh=mesh,
        in_specs=(P("lat", "lon", None), P(), P(), P(), P(), P("lat", "lon", None)),
        out_specs=(
            P("lat", "lon", None),
            P("lat", "lon", None),
            P(None, "lon", None),
            P(None, "lon", None),
            P(),
            P(),
        ),
        check_vma=False,
    )
```

profile of v0, /device:TPU:1, one launch (start us, length us, event | category | flops | bytes accessed | tf_op | source)
XLA Modules:
  0.0 550.6 jit_solution(5417846048986291563)
XLA Ops:
  13.6 3.6 collective-permute-start
  17.2 3.0 collective-permute-start.1
  20.9 6.3 %fusion.108 = (pred[128,308]{0,1:T(8,128)(4,1)S(1)}, pred[128,49,308]{0,1,2:T(8,128)(4,1)S(1)}) fusion(s32[49]{0:T(128)S(1)} %get-tuple-element.67, s32[128,308]{0,1:T(8,128)S(1)} %get-tuple-element.65, s32[49]{0:T(128)S(1)} %get-tuple-element.68, s32[128,308]{0,1:T(8,128)S(1)} %get-tuple-element.66), kind=kLoop, calls=%fused_computation.187 | loop fusion | flops 7687680 | bytes 2286984 | tf_op jit(solution)/shard_map/reduce_or | solution.py:116
  27.2 3.7 fusion.93
  31.0 3.8 fusion.95
  34.7 3.1 compare_and_fusion
  51.5 3.3 fusion.120
  64.5 4.7 collective-permute-start.5
  69.8 6.6 %copy.65 = pred[128,49,308]{2,1,0:T(8,128)(4,1)} copy(pred[128,49,308]{0,1,2:T(8,128)(4,1)S(1)} %get-tuple-element.19) | data formatting | bytes 3863552 | tf_op jit(solution)/shard_map/and | solution.py:51
  82.8 3.2 collective-permute-start.7
  86.0 4.8 convolution_convert_fusion.1
  103.7 3.3 fusion.122
  117.8 4.2 convolution_convert_fusion.2
  127.0 5.1 collective-permute-start.9
  147.8 2.9 pad_maximum_fusion.2
  161.5 3.1 fusion.128
  167.7 3.1 fusion.127
  176.0 3.3 multiply_reduce_fusion.3
  191.1 4.0 convolution_convert_fusion
  198.2 5.1 collective-permute-start.13
  209.3 2.8 collective-permute-start.14
  220.1 2.8 pad_maximum_fusion.3
  236.0 3.0 fusion.130
  242.1 3.2 fusion.129
  252.7 3.2 pad_maximum_fusion
  259.2 3.6 fusion.54
  262.8 3.6 fusion.51
  266.4 3.2 fusion.82
  269.9 53.7 %reduce-scatter.5.cloned.1.call-done = bf16[2,16,1024]{2,1,0:T(8,128)(2,1)} async-done(((bf16[2,512,1024]{2,1,0:T(8,128)(2,1)}), bf16[2,16,1024]{2,1,0:T(8,128)(2,1)}) %reduce-scatter.5.cloned.1.call-update) | async-done | bytes 65552 | tf_op jit(solution)/shard_map/reduce_scatter | solution.py:212
  323.6 128.0 %reduce-scatter.3.cloned.1.call-done = bf16[2,32,1536]{2,1,0:T(8,128)(2,1)} async-done(((bf16[2,1024,1536]{2,1,0:T(8,128)(2,1)}), bf16[2,32,1536]{2,1,0:T(8,128)(2,1)}) %reduce-scatter.3.cloned.1.call-update) | async-done | bytes 196624 | tf_op jit(solution)/shard_map/reduce_scatter | solution.py:209
  451.6 79.9 %all-reduce = (f32[2,1024]{1,0:T(2,128)}, f32[2,8,49]{2,1,0:T(8,128)}) all-reduce(f32[2,1024]{1,0:T(2,128)S(1)} %pad_maximum_fusion.18, f32[2,8,49]{2,1,0:T(8,128)S(1)} %pad_maximum_fusion.19), channel_id=1, replica_groups=mesh['lat'=8,'lon'=32] {'lat','lon'}, use_global_device_ids=true, to_apply=%region_21.22 | all-reduce | flops 2832 | bytes 22656 | tf_op jit(solution)/shard_map/psum | solution.py:220
  532.6 8.0 %all-reduce.4.cloned.1.call-done = (bf16[2,32,1536]{2,1,0:T(8,128)(2,1)}, bf16[2,16,1024]{2,1,0:T(8,128)(2,1)}) async-done(((bf16[2,32,1536]{2,1,0:T(8,128)(2,1)}, bf16[2,16,1024]{2,1,0:T(8,128)(2,1)}), (bf16[2,32,1536]{2,1,0:T(8,128)(2,1)}, bf16[2,16,1024]{2,1,0:T(8,128)(2,1)})) %all-reduce.4.cloned.1.call-update) | async-done | bytes 262160 | tf_op jit(solution)/shard_map/psum | solution.py:217
  (271 shorter events, 160.8 us)
Async XLA Ops:
  7.2 316.4 %reduce-scatter.5.cloned.1.call-start = ((), (), s32[]{:S(2)}) async-start(), calls=%async_computation.3 | async-start | bytes 2162688 | tf_op jit(solution)/shard_map/reduce_scatter | solution.py:212
  13.6 25.0 %collective-permute-start = (bf16[3,16,1024]{2,1,0:T(8,128)(2,1)}, bf16[3,16,1024]{2,1,0:T(8,128)(2,1)S(1)}, u32[]{:S(2)}, u32[]{:S(2)}) collective-permute-start(bf16[3,16,1024]{2,1,0:T(8,128)(2,1)} %get-tuple-element.47), channel_id=1, source_target_pairs={{0,32},{32,64},{64,96},{96,128},{128,160},{160,192},{192,224},{224... | collective-permute-start | bytes 294920 | tf_op jit(solution)/shard_map/ppermute | solution.py:21
  17.2 21.4 %collective-permute-start.1 = (bf16[3,16,1024]{2,1,0:T(8,128)(2,1)}, bf16[3,16,1024]{2,1,0:T(8,128)(2,1)S(1)}, u32[]{:S(2)}, u32[]{:S(2)}) collective-permute-start(bf16[3,16,1024]{2,1,0:T(8,128)(2,1)} %get-tuple-element.48), channel_id=1, source_target_pairs={{32,0},{64,32},{96,64},{128,96},{160,128},{192,160},{224,192},{0,2... | collective-permute-start | bytes 294920 | tf_op jit(solution)/shard_map/ppermute | solution.py:24
  20.9 6.3 %copy-start.48 = (f32[2,8,49]{2,1,0:T(8,128)S(1)}, f32[2,8,49]{2,1,0:T(8,128)}, u32[]{:S(2)}) copy-start(f32[2,8,49]{2,1,0:T(8,128)} %param.10) | copy-start | bytes 9412
  39.3 4.7 collective-permute-start.2
  41.5 4.5 collective-permute-start.3
  60.0 9.3 %copy-start.9 = (bf16[2,512,1024]{2,1,0:T(8,128)(2,1)S(1)}, bf16[2,512,1024]{2,1,0:T(8,128)(2,1)}, u32[]{:S(2)}) copy-start(bf16[2,512,1024]{2,1,0:T(8,128)(2,1)} %param.8) | copy-start | bytes 6291460
  60.0 9.3 %copy-start.39 = (bf16[8,16,1024]{2,1,0:T(8,128)(2,1)S(1)}, bf16[8,16,1024]{2,1,0:T(8,128)(2,1)}, u32[]{:S(2)}) copy-start(bf16[8,16,1024]{2,1,0:T(8,128)(2,1)} %param.11) | copy-start | bytes 786436
  64.2 17.2 %collective-permute-start.4 = (bf16[3,16,1024]{2,1,0:T(8,128)(2,1)}, bf16[3,16,1024]{2,1,0:T(8,128)(2,1)S(1)}, u32[]{:S(2)}, u32[]{:S(2)}) collective-permute-start(bf16[3,16,1024]{2,1,0:T(8,128)(2,1)} %get-tuple-element.45), channel_id=1, source_target_pairs={{0,32},{32,64},{64,96},{96,128},{128,160},{160,192},{192,224},{224... | collective-permute-start | bytes 294920 | tf_op jit(solution)/shard_map/ppermute | solution.py:21
  64.5 16.9 %collective-permute-start.5 = (bf16[3,16,1024]{2,1,0:T(8,128)(2,1)}, bf16[3,16,1024]{2,1,0:T(8,128)(2,1)S(1)}, u32[]{:S(2)}, u32[]{:S(2)}) collective-permute-start(bf16[3,16,1024]{2,1,0:T(8,128)(2,1)} %get-tuple-element.46), channel_id=1, source_target_pairs={{32,0},{64,32},{96,64},{128,96},{160,128},{192,160},{224,192},{0,2... | collective-permute-start | bytes 294920 | tf_op jit(solution)/shard_map/ppermute | solution.py:24
  69.8 7.3 %copy-start.31 = (bf16[8,16,512]{2,1,0:T(8,128)(2,1)}, bf16[8,16,512]{2,1,0:T(8,128)(2,1)S(1)}, u32[]{:S(2)}) copy-start(bf16[8,16,512]{2,1,0:T(8,128)(2,1)S(1)} %convolution_convert_fusion.9) | copy-start | bytes 393220
  69.8 6.6 %copy-start.47 = (bf16[14]{0:T(256)(128)(2,1)S(1)}, bf16[14]{0:T(256)(128)(2,1)}, u32[]{:S(2)}) copy-start(bf16[14]{0:T(256)(128)(2,1)} %get-tuple-element.70) | copy-start | bytes 88
  82.2 12.2 %collective-permute-start.6 = (bf16[14,3,1024]{2,1,0:T(4,128)(2,1)}, bf16[14,3,1024]{2,1,0:T(4,128)(2,1)}, u32[]{:S(2)}, u32[]{:S(2)}) collective-permute-start(bf16[14,3,1024]{2,1,0:T(4,128)(2,1)} %get-tuple-element.41), channel_id=1, source_target_pairs={{0,1},{1,2},{2,3},{3,4},{4,5},{5,6},{6,7},{7,8},{8,9},{9,10},{10,1... | collective-permute-start | bytes 258056 | tf_op jit(solution)/shard_map/ppermute | solution.py:21
  82.8 11.6 %collective-permute-start.7 = (bf16[14,3,1024]{2,1,0:T(4,128)(2,1)}, bf16[14,3,1024]{2,1,0:T(4,128)(2,1)}, u32[]{:S(2)}, u32[]{:S(2)}) collective-permute-start(bf16[14,3,1024]{2,1,0:T(4,128)(2,1)} %get-tuple-element.42), channel_id=1, source_target_pairs={{1,0},{2,1},{3,2},{4,3},{5,4},{6,5},{7,6},{8,7},{9,8},{10,9},{11,1... | collective-permute-start | bytes 258056 | tf_op jit(solution)/shard_map/ppermute | solution.py:24
  97.7 6.0 %copy-start.44 = (pred[128,308]{0,1:T(8,128)(4,1)S(1)}, pred[128,308]{0,1:T(8,128)(4,1)}, u32[]{:S(2)}) copy-start(pred[128,308]{0,1:T(8,128)(4,1)} %broadcast_and_fusion) | copy-start | bytes 118276
  99.2 7.8 %copy-start.15 = (bf16[308,8,64]{0,2,1:T(8,128)(2,1)}, bf16[308,8,64]{0,2,1:T(8,128)(2,1)S(1)}, u32[]{:S(2)}) copy-start(bf16[308,8,64]{0,2,1:T(8,128)(2,1)S(1)} %copy.56) | copy-start | bytes 946180
  127.0 8.1 %collective-permute-start.8 = (bf16[3,16,1808]{2,1,0:T(8,128)(2,1)S(1)}, bf16[3,16,1808]{2,1,0:T(8,128)(2,1)S(1)}, u32[]{:S(2)}, u32[]{:S(2)}) collective-permute-start(bf16[3,16,1808]{2,1,0:T(8,128)(2,1)S(1)} %get-tuple-element.39), channel_id=1, source_target_pairs={{0,32},{32,64},{64,96},{96,128},{128,160},{160,192},{192,224},{224... | collective-permute-start | bytes 520712 | tf_op jit(solution)/shard_map/ppermute | solution.py:21
  127.0 8.5 %collective-permute-start.9 = (bf16[3,16,1808]{2,1,0:T(8,128)(2,1)S(1)}, bf16[3,16,1808]{2,1,0:T(8,128)(2,1)S(1)}, u32[]{:S(2)}, u32[]{:S(2)}) collective-permute-start(bf16[3,16,1808]{2,1,0:T(8,128)(2,1)S(1)} %get-tuple-element.40), channel_id=1, source_target_pairs={{32,0},{64,32},{96,64},{128,96},{160,128},{192,160},{224,192},{0,2... | collective-permute-start | bytes 520712 | tf_op jit(solution)/shard_map/ppermute | solution.py:24
  134.6 7.1 %copy-start.2 = (bf16[8,128,308]{1,2,0:T(8,128)(2,1)S(1)}, bf16[8,128,308]{1,2,0:T(8,128)(2,1)}, u32[]{:S(2)}) copy-start(bf16[8,128,308]{1,2,0:T(8,128)(2,1)} %get-tuple-element.16) | copy-start | bytes 1892356
  134.6 7.1 %copy-start.16 = (bf16[308,8,64]{0,2,1:T(8,128)(2,1)S(1)}, bf16[308,8,64]{0,2,1:T(8,128)(2,1)}, u32[]{:S(2)}) copy-start(bf16[308,8,64]{0,2,1:T(8,128)(2,1)} %copy-done.15) | copy-start | bytes 946180
  136.7 11.1 %collective-permute-start.10 = (bf16[14,3,1808]{2,1,0:T(4,128)(2,1)}, bf16[14,3,1808]{2,1,0:T(4,128)(2,1)}, u32[]{:S(2)}, u32[]{:S(2)}) collective-permute-start(bf16[14,3,1808]{2,1,0:T(4,128)(2,1)} %get-tuple-element.31), channel_id=1, source_target_pairs={{0,1},{1,2},{2,3},{3,4},{4,5},{5,6},{6,7},{7,8},{8,9},{9,10},{10,1... | collective-permute-start | bytes 455624 | tf_op jit(solution)/shard_map/ppermute | solution.py:21
  139.3 8.5 %collective-permute-start.11 = (bf16[14,3,1808]{2,1,0:T(4,128)(2,1)}, bf16[14,3,1808]{2,1,0:T(4,128)(2,1)}, u32[]{:S(2)}, u32[]{:S(2)}) collective-permute-start(bf16[14,3,1808]{2,1,0:T(4,128)(2,1)} %get-tuple-element.32), channel_id=1, source_target_pairs={{1,0},{2,1},{3,2},{4,3},{5,4},{6,5},{7,6},{8,7},{9,8},{10,9},{11,1... | collective-permute-start | bytes 455624 | tf_op jit(solution)/shard_map/ppermute | solution.py:24
  198.0 8.5 %collective-permute-start.12 = (bf16[3,16,1808]{2,1,0:T(8,128)(2,1)}, bf16[3,16,1808]{2,1,0:T(8,128)(2,1)}, u32[]{:S(2)}, u32[]{:S(2)}) collective-permute-start(bf16[3,16,1808]{2,1,0:T(8,128)(2,1)} %get-tuple-element.37), channel_id=1, source_target_pairs={{0,32},{32,64},{64,96},{96,128},{128,160},{160,192},{192,224},{224... | collective-permute-start | bytes 520712 | tf_op jit(solution)/shard_map/ppermute | solution.py:21
  198.2 6.5 %copy-start.25 = (bf16[1,512,1024]{2,1,0:T(8,128)(2,1)S(1)}, bf16[1,512,1024]{2,1,0:T(8,128)(2,1)}, u32[]{:S(2)}) copy-start(bf16[1,512,1024]{2,1,0:T(8,128)(2,1)} %fusion.31) | copy-start | bytes 3145732
  198.2 9.1 %collective-permute-start.13 = (bf16[3,16,1808]{2,1,0:T(8,128)(2,1)}, bf16[3,16,1808]{2,1,0:T(8,128)(2,1)}, u32[]{:S(2)}, u32[]{:S(2)}) collective-permute-start(bf16[3,16,1808]{2,1,0:T(8,128)(2,1)} %get-tuple-element.38), channel_id=1, source_target_pairs={{32,0},{64,32},{96,64},{128,96},{160,128},{192,160},{224,192},{0,2... | collective-permute-start | bytes 520712 | tf_op jit(solution)/shard_map/ppermute | solution.py:24
  206.3 245.3 %reduce-scatter.3.cloned.1.call-start = ((), (), s32[]{:S(2)}) async-start(), calls=%async_computation.2 | async-start | bytes 6488064 | tf_op jit(solution)/shard_map/reduce_scatter | solution.py:209
  206.4 7.6 %copy-start.1 = (bf16[8,128,308]{1,2,0:T(8,128)(2,1)S(1)}, bf16[8,128,308]{1,2,0:T(8,128)(2,1)}, u32[]{:S(2)}) copy-start(bf16[8,128,308]{1,2,0:T(8,128)(2,1)} %get-tuple-element.14) | copy-start | bytes 1892356
  206.4 7.6 %copy-start.12 = (bf16[308,8,64]{0,2,1:T(8,128)(2,1)S(1)}, bf16[308,8,64]{0,2,1:T(8,128)(2,1)}, u32[]{:S(2)}) copy-start(bf16[308,8,64]{0,2,1:T(8,128)(2,1)} %copy-done.11) | copy-start | bytes 946180
  209.3 10.8 %collective-permute-start.14 = (bf16[14,3,1808]{2,1,0:T(4,128)(2,1)}, bf16[14,3,1808]{2,1,0:T(4,128)(2,1)}, u32[]{:S(2)}, u32[]{:S(2)}) collective-permute-start(bf16[14,3,1808]{2,1,0:T(4,128)(2,1)} %get-tuple-element.29), channel_id=1, source_target_pairs={{0,1},{1,2},{2,3},{3,4},{4,5},{5,6},{6,7},{7,8},{8,9},{9,10},{10,1... | collective-permute-start | bytes 455624 | tf_op jit(solution)/shard_map/ppermute | solution.py:21
  212.1 8.0 %collective-permute-start.15 = (bf16[14,3,1808]{2,1,0:T(4,128)(2,1)}, bf16[14,3,1808]{2,1,0:T(4,128)(2,1)}, u32[]{:S(2)}, u32[]{:S(2)}) collective-permute-start(bf16[14,3,1808]{2,1,0:T(4,128)(2,1)} %get-tuple-element.30), channel_id=1, source_target_pairs={{1,0},{2,1},{3,2},{4,3},{5,4},{6,5},{7,6},{8,7},{9,8},{10,9},{11,1... | collective-permute-start | bytes 455624 | tf_op jit(solution)/shard_map/ppermute | solution.py:24
  255.9 284.6 %all-reduce.4.cloned.1.call-start = ((), (), s32[]{:S(2)}) async-start(), calls=%async_computation.4 | async-start | bytes 524288 | tf_op jit(solution)/shard_map/psum | solution.py:217
  266.4 265.2 %copy-start.24 = (bf16[8,16,1024]{2,1,0:T(8,128)(2,1)S(1)}, bf16[8,16,1024]{2,1,0:T(8,128)(2,1)}, u32[]{:S(2)}) copy-start(bf16[8,16,1024]{2,1,0:T(8,128)(2,1)} %copy-done.23) | copy-start | bytes 786436
  (36 other events, 87.9 us)
Sparse Core Ops, SparseCore 0:
  206.4 117.1 reduce-scatter.4
  326.3 125.1 reduce-scatter.2
  454.5 86.0 all-reduce.3
where the time goes:
time: 559 us; the launch traced here: 551 us
  waiting for transfers between devices  194 us (35%)
  local copies, waits for them, and re-layouts  96.4 us (17%)
  matrix products  83.5 us (15%)
  blocking collectives  79.9 us (14%)
  other arithmetic  43.5 us (8%)
  starting transfers between devices  38.9 us (7%)
  between operations  14.8 us (3%)
    reduce_scatter x1, waiting for transfers between devices, shards(): lax.psum_scatter(jnp.stack(packed_terms).astype(jnp.bfloat16), 'lon', sca...  128 us
    psum x1, blocking collectives, shards(): lax.psum((jnp.stack(gain_terms), jnp.stack(bias_terms)), ('lat', 'lon'))  79.9 us
    reduce_scatter x1, waiting for transfers between devices, shards(): lax.psum_scatter(jnp.stack(output_terms).astype(jnp.bfloat16), 'lon', sca...  53.7 us
    ppermute x8, starting transfers between devices, extended(): lax.ppermute(lax.slice_in_dim(block, 0, width, axis=dim), axis, backward)  26.1 us
    ppermute x8, starting transfers between devices, extended(): lax.ppermute(lax.slice_in_dim(block, block.shape[dim] - width, None, axis...  12.4 us
    unnamed x102, local copies, waits for them, and re-layouts  12 us
  transfers between devices with their start and end apart: 19, of which 8 were waited for; matrix products, arithmetic and copies ran while one was open for 20% of the time, Pallas kernels for 0%

commit v1 on v0

v1 whole, which is shorter than its diff:
```python
import functools

import jax
import jax.numpy as jnp
import numpy as np
from jax import lax
from jax.experimental import pallas as pl
from jax.experimental.pallas import tpu as pltpu
from jax.sharding import PartitionSpec as P

HEADS = 8
HEAD_DIM = 64
WIN = 7
RADIUS = 3
LAYERS = 2
D = 1024
INNER = 512
ROWS, COLS = 8, 16
CELLS = ROWS * COLS
KEYS = 352
EPS = 1e-05
MESH = pl.DeviceIdType.MESH
F32, BF16 = jnp.float32, jnp.bfloat16

SEGMENTS = (
    (128, 48, -1, 0),
    (176, 48, 1, 0),
    (224, 32, 0, -1),
    (256, 32, 0, 1),
    (288, 16, -1, -1),
    (304, 16, -1, 1),
    (320, 16, 1, -1),
    (336, 16, 1, 1),
)


def geometry():
    key_coord = np.full((8, KEYS), 1000, np.int32)
    select = np.zeros((128, CELLS), np.float32)
    for i in range(ROWS):
        for j in range(COLS):
            key_coord[0, i * COLS + j], key_coord[1, i * COLS + j] = i, j
    for first, _, d_lat, d_lon in SEGMENTS:
        rows = {-1: range(5, 8), 0: range(8), 1: range(3)}[d_lat]
        cols = {-1: range(13, 16), 0: range(16), 1: range(3)}[d_lon]
        place = first
        for i in rows:
            for j in cols:
                key_coord[0, place], key_coord[1, place] = i + d_lat * ROWS, j + d_lon * COLS
                if d_lon != 0:
                    select[place - 224, i * COLS + j] = 1.0
                place += 1
    return key_coord, select


KEY_COORD, SELECT = geometry()


def place():
    return lax.axis_index("lat"), lax.axis_index("lon")


def at(lat, lon, d_lat, d_lon):
    return (lax.rem(lat + d_lat + 8, 8), lax.rem(lon + d_lon + 32, 32))


def greet(lat, lon):
    barrier = pltpu.get_barrier_semaphore()
    for _, _, d_lat, d_lon in SEGMENTS:
        pl.semaphore_signal(
            barrier, inc=1, device_id=at(lat, lon, d_lat, d_lon), device_id_type=MESH
        )
    return barrier


def dot(a, b, dims=((1,), (0,))):
    return lax.dot_general(a, b, (dims, ((), ())), preferred_element_type=F32)


def norm_parts(x):
    mean = jnp.mean(x, axis=-1, keepdims=True)
    centred = x - mean
    var = jnp.mean(centred * centred, axis=-1, keepdims=True)
    return centred, lax.rsqrt(var + EPS)


def split_heads(pair):
    low = lax.broadcasted_iota(jnp.int32, pair.shape, 1) < HEAD_DIM
    zero = jnp.zeros_like(pair)
    return jnp.concatenate([jnp.where(low, pair, zero), jnp.where(low, zero, pair)], axis=0)


def join_heads(both):
    low = lax.broadcasted_iota(jnp.int32, (CELLS, 2 * HEAD_DIM), 1) < HEAD_DIM
    return jnp.where(low, both[:CELLS], both[CELLS:])


def fwd_kernel(
    x_ref, win_ref, wout_ref, gain_ref, bias_ref, sel_ref, coord_ref,
    y_ref, normed_ref, q_ref, kv_ref, p_ref, mixed_ref,
    pack_ref, rw_ref, dense_ref, send_sem, recv_sem,
):
    lat, lon = place()
    barrier = greet(lat, lon)
    x = x_ref[...].astype(F32)
    centred, rstd = norm_parts(x)
    normed = (centred * rstd * gain_ref[...]).astype(BF16)
    normed_ref[...] = normed
    kv = dot(normed, win_ref[:, INNER:]).astype(BF16)
    kv_ref[0:CELLS, :] = kv
    pack_ref[...] = dot(sel_ref[...], kv).astype(BF16)
    pl.semaphore_wait(barrier, len(SEGMENTS))
    copies = []
    for n, (first, rows, d_lat, d_lon) in enumerate(SEGMENTS):
        if d_lon == 0:
            source = kv_ref.at[pl.ds(80 if d_lat < 0 else 0, rows)]
        else:
            source = pack_ref.at[pl.ds(first - 224, rows)]
        copy = pltpu.make_async_remote_copy(
            src_ref=source,
            dst_ref=kv_ref.at[pl.ds(first, rows)],
            send_sem=send_sem.at[n],
            recv_sem=recv_sem.at[n],
            device_id=at(lat, lon, -d_lat, -d_lon),
            device_id_type=MESH,
        )
        copy.start()
        copies.append(copy)
    q_ref[...] = dot(normed, win_ref[:, :INNER]).astype(BF16)
    key_i = coord_ref[0:1, :]
    row_ok = (lat * ROWS + key_i >= 0) & (lat * ROWS + key_i < 64)
    step_lat = jnp.where(row_ok, key_i, 1000) - lax.broadcasted_iota(jnp.int32, (ROWS, KEYS), 0)
    step_lon = coord_ref[1:2, :] - lax.broadcasted_iota(jnp.int32, (COLS, KEYS), 0)

    def expand(head, _):
        for w in range(WIN):
            acc = jnp.full((ROWS, KEYS), -jnp.inf, F32)
            for u in range(WIN):
                acc = jnp.where(step_lat == u - RADIUS, bias_ref[head, u * WIN + w], acc)
            rw_ref[w] = acc
        for i in range(ROWS):
            acc = jnp.full((COLS, KEYS), -jnp.inf, F32)
            for w in range(WIN):
                acc = jnp.where(step_lon == w - RADIUS, rw_ref[w, i : i + 1, :], acc)
            dense_ref[head, i * COLS : (i + 1) * COLS, :] = acc
        return 0

    lax.fori_loop(0, HEADS, expand, 0)
    for copy in copies:
        copy.wait()
    for pair in range(HEADS // 2):
        lanes = slice(pair * 128, pair * 128 + 128)
        queries = split_heads(q_ref[:, lanes])
        bias = dense_ref[2 * pair : 2 * pair + 2].reshape(2 * CELLS, KEYS)
        scores = dot(queries, kv_ref[:, lanes], ((1,), (1,))) * HEAD_DIM ** (-0.5) + bias
        top = jnp.max(scores, axis=-1, keepdims=True)
        weight = jnp.exp(scores - top)
        probs = weight / jnp.sum(weight, axis=-1, keepdims=True)
        p_ref[2 * pair : 2 * pair + 2] = probs.reshape(2, CELLS, KEYS)
        values = kv_ref[:, INNER + pair * 128 : INNER + pair * 128 + 128]
        mixed_ref[:, lanes] = join_heads(dot(probs.astype(BF16), values)).astype(BF16)
    y_ref[...] = (x + dot(mixed_ref[...], wout_ref[...])).astype(BF16)


def bwd_kernel(
    up_ref, x_ref, q_ref, kv_ref, p_ref, win_ref, wout_ref, gain_ref, sel_ref, coord_ref,
    down_ref, gp_ref, gain_grad_ref, bias_grad_ref,
    part_ref, out_ref, in_ref, ds_ref, sums_ref, send_sem, recv_sem,
):
    lat, lon = place()
    barrier = greet(lat, lon)
    up = up_ref[...]
    grad_mixed = dot(up, wout_ref[...], ((1,), (1,))).astype(BF16)
    scale = HEAD_DIM ** (-0.5)
    for pair in range(HEADS // 2):
        lanes = slice(pair * 128, pair * 128 + 128)
        vlanes = slice(INNER + pair * 128, INNER + pair * 128 + 128)
        keys = kv_ref[:, lanes]
        grads = split_heads(grad_mixed[:, lanes])
        grad_probs = dot(grads, kv_ref[:, vlanes], ((1,), (1,)))
        probs = p_ref[2 * pair : 2 * pair + 2].reshape(2 * CELLS, KEYS)
        delta = jnp.sum(probs * grad_probs, axis=-1, keepdims=True)
        grad_scores = probs * (grad_probs - delta)
        ds_ref[2 * pair : 2 * pair + 2] = grad_scores.reshape(2, CELLS, KEYS)
        scores_low = grad_scores.astype(BF16)
        gp_ref[:, lanes] = (join_heads(dot(scores_low, keys)) * scale).astype(BF16)
        grad_keys = dot(scores_low, split_heads(q_ref[:, lanes]), ((0,), (0,))) * scale
        grad_values = dot(probs.astype(BF16), grads, ((0,), (0,)))
        part_ref[:, lanes] = grad_keys[:CELLS]
        part_ref[:, vlanes] = grad_values[:CELLS]
        out_ref[:, lanes] = grad_keys[CELLS:].astype(BF16)
        out_ref[:, vlanes] = grad_values[CELLS:].astype(BF16)
    pl.semaphore_wait(barrier, len(SEGMENTS))
    copies = []
    for n, (first, rows, d_lat, d_lon) in enumerate(SEGMENTS):
        copy = pltpu.make_async_remote_copy(
            src_ref=out_ref.at[pl.ds(first - 128, rows)],
            dst_ref=in_ref.at[pl.ds(first - 128, rows)],
            send_sem=send_sem.at[n],
            recv_sem=recv_sem.at[n],
            device_id=at(lat, lon, d_lat, d_lon),
            device_id_type=MESH,
        )
        copy.start()
        copies.append(copy)
    key_i = jnp.broadcast_to(coord_ref[0:1, :], (COLS, KEYS))
    step_lon = coord_ref[1:2, :] - lax.broadcasted_iota(jnp.int32, (COLS, KEYS), 0)
    ones = jnp.ones((8, KEYS), F32)
    sums_ref[...] = jnp.zeros_like(sums_ref)

    def collect(head, _):
        for u in range(WIN):
            acc = jnp.zeros((COLS, KEYS), F32)
            for i in range(ROWS):
                acc += jnp.where(
                    key_i == i + u - RADIUS, ds_ref[head, i * COLS : (i + 1) * COLS, :], 0.0
                )
            for w in range(WIN):
                o = u * WIN + w
                sums_ref[o : o + 1, :] = jnp.sum(
                    jnp.where(step_lon == w - RADIUS, acc, 0.0), axis=0, keepdims=True
                )
        total = lax.dot_general(
            ones, sums_ref[...], (((1,), (1,)), ((), ())),
            precision=lax.Precision.HIGHEST, preferred_element_type=F32,
        )
        bias_grad_ref[head] = total
        return 0

    lax.fori_loop(0, HEADS, collect, 0)
    for copy in copies:
        copy.wait()
    part_ref[80:128, :] += in_ref[0:48, :].astype(F32)
    part_ref[0:48, :] += in_ref[48:96, :].astype(F32)
    total = part_ref[...] + dot(sel_ref[...], in_ref[96:224, :], ((0,), (0,)))
    gp_ref[:, INNER:] = total.astype(BF16)
    grad_normed = dot(gp_ref[...], win_ref[...], ((1,), (1,)))
    centred, rstd = norm_parts(x_ref[...].astype(F32))
    unit = centred * rstd
    gain_grad_ref[...] = jnp.sum(grad_normed * unit, axis=0, keepdims=True)
    scaled = grad_normed * gain_ref[...]
    mean_a = jnp.mean(scaled, axis=-1, keepdims=True)
    mean_b = jnp.mean(scaled * unit, axis=-1, keepdims=True)
    down_ref[...] = (up.astype(F32) + rstd * (scaled - mean_a - unit * mean_b)).astype(BF16)


def vmem(count):
    return [pl.BlockSpec(memory_space=pltpu.VMEM)] * count


def params(collective_id):
    return pltpu.CompilerParams(
        collective_id=collective_id, has_side_effects=True, vmem_limit_bytes=48 * 1024 * 1024
    )


def shape(dims, dtype):
    return jax.ShapeDtypeStruct(dims, dtype)


def fwd_layer(x, win, wout, gain, bias, sel, coord):
    return pl.pallas_call(
        fwd_kernel,
        out_shape=(
            shape((CELLS, D), BF16),
            shape((CELLS, D), BF16),
            shape((CELLS, INNER), BF16),
            shape((KEYS, D), BF16),
            shape((HEADS, CELLS, KEYS), F32),
            shape((CELLS, INNER), BF16),
        ),
        in_specs=vmem(4) + [pl.BlockSpec(memory_space=pltpu.SMEM)] + vmem(2),
        out_specs=tuple(vmem(6)),
        scratch_shapes=[
            pltpu.VMEM((128, D), BF16),
            pltpu.VMEM((WIN, ROWS, KEYS), F32),
            pltpu.VMEM((HEADS, CELLS, KEYS), F32),
            pltpu.SemaphoreType.DMA((8,)),
            pltpu.SemaphoreType.DMA((8,)),
        ],
        compiler_params=params(0),
    )(x, win, wout, gain, bias, sel, coord)


def bwd_layer(up, x, q, kv, p, win, wout, gain, sel, coord):
    return pl.pallas_call(
        bwd_kernel,
        out_shape=(
            shape((CELLS, D), BF16),
            shape((CELLS, 3 * INNER), BF16),
            shape((1, D), F32),
            shape((HEADS, 8, 56), F32),
        ),
        in_specs=vmem(10),
        out_specs=tuple(vmem(4)),
        scratch_shapes=[
            pltpu.VMEM((CELLS, D), F32),
            pltpu.VMEM((KEYS - CELLS, D), BF16),
            pltpu.VMEM((KEYS - CELLS, D), BF16),
            pltpu.VMEM((HEADS, CELLS, KEYS), F32),
            pltpu.VMEM((56, KEYS), F32),
            pltpu.SemaphoreType.DMA((8,)),
            pltpu.SemaphoreType.DMA((8,)),
        ],
        compiler_params=params(1),
    )(up, x, q, kv, p, win, wout, gain, sel, coord)


def shards(inputs, input_weight, output_weight, norm_gain, position_bias, cotangent):
    sel = jnp.asarray(SELECT, BF16)
    coord = jnp.asarray(KEY_COORD)
    stream = inputs.reshape(CELLS, D)
    stored = []
    for l in range(LAYERS):
        y, normed, q, kv, p, mixed = fwd_layer(
            stream, input_weight[l], output_weight[l], norm_gain[l : l + 1], position_bias[l], sel, coord
        )
        stored.append((stream, normed, q, kv, p, mixed))
        stream = y
    up = cotangent.reshape(CELLS, D)
    packed_terms, output_terms = [None] * LAYERS, [None] * LAYERS
    gain_terms, bias_terms = [None] * LAYERS, [None] * LAYERS
    for l in reversed(range(LAYERS)):
        x, normed, q, kv, p, mixed = stored[l]
        output_terms[l] = dot(mixed, up, ((0,), (0,)))
        up, gp, gain_grad, bias_grad = bwd_layer(
            up, x, q, kv, p, input_weight[l], output_weight[l], norm_gain[l : l + 1], sel, coord
        )
        packed_terms[l] = dot(normed, gp, ((0,), (0,)))
        gain_terms[l] = gain_grad[0]
        bias_terms[l] = bias_grad[:, 0, : WIN * WIN]
    lon_share = (
        lax.psum_scatter(
            jnp.stack(packed_terms).astype(jnp.bfloat16), "lon", scatter_dimension=1, tiled=True
        ),
        lax.psum_scatter(
            jnp.stack(output_terms).astype(jnp.bfloat16), "lon", scatter_dimension=1, tiled=True
        ),
    )
    packed_grad, output_grad = (
        lax.psum(lon_share[0], "lat").astype(F32),
        lax.psum(lon_share[1], "lat").astype(F32),
    )
    gain_grad, bias_grad = lax.psum((jnp.stack(gain_terms), jnp.stack(bias_terms)), ("lat", "lon"))
    tile = (ROWS, COLS, D)
    return (stream.reshape(tile), up.reshape(tile), packed_grad, output_grad, gain_grad, bias_grad)


def solution(mesh):
    return jax.shard_map(
        shards,
        mesh=mesh,
        in_specs=(P("lat", "lon", None), P(), P(), P(), P(), P("lat", "lon", None)),
        out_specs=(
            P("lat", "lon", None),
            P("lat", "lon", None),
            P(None, "lon", None),
            P(None, "lon", None),
            P(),
            P(),
        ),
        check_vma=False,
    )
```

time: 559 us -> 425 us (0.76)
  local copies, waits for them, and re-layouts: 96.4 us -> 14.2 us
  matrix products: 83.5 us -> 2.91 us
  Pallas kernels: 0 us -> 75.8 us
  starting transfers between devices: 38.9 us -> 0.3 us
  other arithmetic: 43.5 us -> 7.98 us
  waiting for transfers between devices: 194 us -> 225 us
    pallas_call x0 -> x4, Pallas kernels: none -> 75.8 us  [the longest x2 39.7 us: fwd_layer(): pl.pallas_call(fwd_kernel, out_shape=(shape((CELLS, D), BF16), shape((CEL...]
    dot_general x34 -> x4, matrix products: 76.9 us -> 2.91 us  [dot(): return lax.dot_general(a, b, (dims, ((), ())), preferred_element_type=F32)]
    ppermute x16 -> x0, starting transfers between devices: 38.5 us -> none  [the longest x8 26.1 us: extended(): lax.ppermute(lax.slice_in_dim(block, 0, width, axis=dim), axis, backward)]
    reduce_scatter x1, waiting for transfers between devices: 53.7 us -> 89 us  [shards(): lax.psum_scatter(jnp.stack(output_terms).astype(jnp.bfloat16), 'lon', sca...]
    reshape x30 -> x0, local copies, waits for them, and re-layouts: 34 us -> none  [the longest x4 7.23 us: attend(): value_heads = values_wide.reshape(-1, HEADS, HEAD_DIM)]
    concatenate x8 -> x0, local copies, waits for them, and re-layouts: 14 us -> none  [the longest x4 10.2 us: extended(): block = jnp.concatenate([low, block, high], axis=dim)]
    convert_element_type x8 -> x0, local copies, waits for them, and re-layouts: 11.2 us -> none  [the longest x2 4.85 us: shards(): scores_low = grad_scores.astype(jnp.bfloat16)]
    slice x15 -> x2, local copies, waits for them, and re-layouts: 11.2 us -> 0.79 us  [the longest x1 0.78 us: shards(): norm_gain[l:l + 1]]
  transfers between devices with their start and end apart: 19 -> 3, of which waited for: 8 -> 3; matrix products, arithmetic and copies ran while one was open for 20% -> 1% of each run, Pallas kernels for 0% -> 4%
where the time goes in v1:
time: 425 us; the launch traced here: 421 us
  waiting for transfers between devices  225 us (53%)
  blocking collectives  80.1 us (19%)
  Pallas kernels  75.8 us (18%)
  local copies, waits for them, and re-layouts  14.2 us (3%)
  between operations  14 us (3%)
  other arithmetic  7.98 us (2%)
    reduce_scatter x1, waiting for transfers between devices, shards(): lax.psum_scatter(jnp.stack(packed_terms).astype(jnp.bfloat16), 'lon', sca...  128 us
    reduce_scatter x1, waiting for transfers between devices, shards(): lax.psum_scatter(jnp.stack(output_terms).astype(jnp.bfloat16), 'lon', sca...  89 us
    psum x1, blocking collectives, shards(): lax.psum((jnp.stack(gain_terms), jnp.stack(bias_terms)), ('lat', 'lon'))  80.1 us
    pallas_call x2, Pallas kernels, fwd_layer(): pl.pallas_call(fwd_kernel, out_shape=(shape((CELLS, D), BF16), shape((CEL...  39.7 us
    pallas_call x2, Pallas kernels, bwd_layer(): pl.pallas_call(bwd_kernel, out_shape=(shape((CELLS, D), BF16), shape((CEL...  36.2 us
    psum x1, waiting for transfers between devices, shards(): lax.psum(lon_share[0], 'lat').astype(F32)  8.75 us
  transfers between devices with their start and end apart: 3, of which 3 were waited for; matrix products, arithmetic and copies ran while one was open for 1% of the time, Pallas kernels for 4%

profile of v1, /device:TPU:1, one launch (start us, length us, event | category | flops | bytes accessed | tf_op | source)
XLA Modules:
  0.0 420.6 jit_solution(8326567526553368540)
XLA Ops:
  7.2 0.0 reduce-scatter.5.cloned.1.call-start
  7.2 0.8 fusion.4
  8.0 0.7 slice_bitcast_fusion.5
  8.7 1.7 slice_bitcast_fusion.2
  10.5 5.9 %slice_bitcast_fusion = (bf16[1024,1536]{1,0:T(8,128)(2,1)}, bf16[1024,1536]{1,0:T(8,128)(2,1)}) fusion(bf16[2,1024,1536]{2,1,0:T(8,128)(2,1)} %param.9), kind=kLoop, calls=%fused_computation.5 | loop fusion | bytes 12582912 | tf_op jit(solution)/shard_map/squeeze | solution.py:316
  16.3 21.2 %shard_map.127 = (bf16[128,1024]{1,0:T(8,128)(2,1)S(1)}, bf16[128,1024]{1,0:T(8,128)(2,1)S(1)}, bf16[128,512]{1,0:T(8,128)(2,1)S(1)}, bf16[352,1024]{1,0:T(8,128...) custom-call(bf16[128,1024]{1,0:T(8,128)(2,1)S(1)} %bitcast.35, ...), custom_call_target="tpu_custom_call" | custom-call | tf_op jit(solution)/shard_map/pallas_call | solution.py:262
  37.5 0.6 copy-done.14
  38.2 18.5 %shard_map.128 = (bf16[128,1024]{1,0:T(8,128)(2,1)S(1)}, bf16[128,1024]{1,0:T(8,128)(2,1)S(1)}, bf16[128,512]{1,0:T(8,128)(2,1)S(1)}, bf16[352,1024]{1,0:T(8,128...) custom-call(bf16[128,1024]{1,0:T(8,128)(2,1)S(1)} %get-tuple-element.26.x_ref, ...), custom_call_target="tpu_custom_call" | custom-call | tf_op jit(solution)/shard_map/pallas_call | solution.py:262
  56.7 0.4 fusion.3
  57.2 0.2 copy-done.11
  57.4 18.6 %shard_map.129 = (bf16[128,1024]{1,0:T(8,128)(2,1)S(1)}, bf16[128,1536]{1,0:T(8,128)(2,1)S(1)}, f32[1,1024]{1,0:T(1,128)S(1)}, f32[8,8,56]{2,1,0:T(8,128)S(1)}) custom-call(bf16[128,1024]{1,0:T(8,128)(2,1)S(1)} %bitcast.38, bf16[128,1024]{1,0:T(8,128)(2,1)S(1)} %get-tuple-element.26.x_ref, bf16[128,512]{1,0:T(8,128)(2,1)S(1)} %get-tuple-element.28.q_ref, ...), custom_call_target="tpu_custom_call" | custom-call | tf_op jit(solution)/shard_map/pallas_call | solution.py:286
  76.0 0.7 copy-done.5
  76.7 0.5 fusion.2
  77.2 1.6 pad_maximum_fusion.1
  78.7 0.0 reduce-scatter.5.cloned.1.call-update
  78.7 0.2 reduce-scatter.3.cloned.1.call-start
  79.0 1.1 copy-done.3
  80.1 0.9 copy-done.15
  81.0 17.6 %shard_map.130 = (bf16[128,1024]{1,0:T(8,128)(2,1)S(1)}, bf16[128,1536]{1,0:T(8,128)(2,1)S(1)}, f32[1,1024]{1,0:T(1,128)S(1)}, f32[8,8,56]{2,1,0:T(8,128)S(1)}) custom-call(bf16[128,1024]{1,0:T(8,128)(2,1)S(1)} %get-tuple-element.31.up_ref, bf16[128,1024]{1,0:T(8,128)(2,1)S(1)} %bitcast.36, bf16[128,512]{1,0:T(8,128)(2,1)S(1)} %copy-done.15, ...), custom_call_target="tpu_custom_call" | custom-call | tf_op jit(solution)/shard_map/pallas_call | solution.py:286
  98.6 1.0 fusion.1
  99.7 1.0 fusion
  100.7 3.2 pad_maximum_fusion
  103.9 0.0 reduce-scatter.3.cloned.1.call-update
  103.9 0.0 all-reduce.4.cloned.1.call-start
  104.0 89.0 %reduce-scatter.5.cloned.1.call-done = bf16[2,16,1024]{2,1,0:T(8,128)(2,1)} async-done(((bf16[2,512,1024]{2,1,0:T(8,128)(2,1)}), bf16[2,16,1024]{2,1,0:T(8,128)(2,1)}) %reduce-scatter.5.cloned.1.call-update) | async-done | bytes 65552 | tf_op jit(solution)/shard_map/reduce_scatter | solution.py:336
  193.0 127.5 %reduce-scatter.3.cloned.1.call-done = bf16[2,32,1536]{2,1,0:T(8,128)(2,1)} async-done(((bf16[2,1024,1536]{2,1,0:T(8,128)(2,1)}), bf16[2,32,1536]{2,1,0:T(8,128)(2,1)}) %reduce-scatter.3.cloned.1.call-update) | async-done | bytes 196624 | tf_op jit(solution)/shard_map/reduce_scatter | solution.py:333
  320.6 80.1 %all-reduce = (f32[2,1024]{1,0:T(2,128)}, f32[2,8,49]{2,1,0:T(8,128)}) all-reduce(f32[2,1024]{1,0:T(2,128)S(1)} %pad_maximum_fusion.2, f32[2,8,49]{2,1,0:T(8,128)S(1)} %pad_maximum_fusion.3), channel_id=1, replica_groups=mesh['lat'=8,'lon'=32] {'lat','lon'}, use_global_device_ids=true, to_apply=%region_4.0 | all-reduce | flops 2832 | bytes 22656 | tf_op jit(solution)/shard_map/psum | solution.py:344
  400.7 8.8 %all-reduce.4.cloned.1.call-done = (bf16[2,32,1536]{2,1,0:T(8,128)(2,1)}, bf16[2,16,1024]{2,1,0:T(8,128)(2,1)}) async-done(((bf16[2,32,1536]{2,1,0:T(8,128)(2,1)}, bf16[2,16,1024]{2,1,0:T(8,128)(2,1)}), (bf16[2,32,1536]{2,1,0:T(8,128)(2,1)}, bf16[2,16,1024]{2,1,0:T(8,128)(2,1)})) %all-reduce.4.cloned.1.call-update) | async-done | bytes 262160 | tf_op jit(solution)/shard_map/psum | solution.py:341
  409.5 1.5 convert_element_type.9
  411.0 1.7 convert_element_type.8
  412.7 0.7 copy.19
  413.4 0.7 copy.20
  (33 shorter events, 0.1 us)
Async XLA Ops:
  7.2 185.8 %reduce-scatter.5.cloned.1.call-start = ((), (), s32[]{:S(2)}) async-start(), calls=%async_computation.3 | async-start | bytes 2162688 | tf_op jit(solution)/shard_map/reduce_scatter | solution.py:336
  10.4 5.9 %copy-start = (bf16[8,16,1024]{2,1,0:T(8,128)(2,1)S(1)}, bf16[8,16,1024]{2,1,0:T(8,128)(2,1)}, u32[]{:S(2)}) copy-start(bf16[8,16,1024]{2,1,0:T(8,128)(2,1)} %param.8) | copy-start | bytes 786436
  10.4 5.9 %copy-start.4 = (bf16[128,128]{1,0:T(8,128)(2,1)S(1)}, bf16[128,128]{1,0:T(8,128)(2,1)}, u32[]{:S(2)}) copy-start(bf16[128,128]{1,0:T(8,128)(2,1)} %constant.4.clone.sel_ref) | copy-start | bytes 98308
  10.4 5.9 %copy-start.13 = (s32[8,352]{1,0:T(8,128)S(1)}, s32[8,352]{1,0:T(8,128)}, u32[]{:S(2)}) copy-start(s32[8,352]{1,0:T(8,128)} %constant.5.clone.coord_ref) | copy-start | bytes 33796
  37.5 0.7 copy-start.14
  38.2 19.0 %copy-start.9 = (bf16[128,1024]{1,0:T(8,128)(2,1)}, bf16[128,1024]{1,0:T(8,128)(2,1)S(1)}, u32[]{:S(2)}) copy-start(bf16[128,1024]{1,0:T(8,128)(2,1)S(1)} %get-tuple-element.36) | copy-start | bytes 786436
  38.2 37.8 %copy-start.2 = (bf16[352,1024]{1,0:T(8,128)(2,1)}, bf16[352,1024]{1,0:T(8,128)(2,1)S(1)}, u32[]{:S(2)}) copy-start(bf16[352,1024]{1,0:T(8,128)(2,1)S(1)} %get-tuple-element.33.kv_ref) | copy-start | bytes 2162692
  38.2 18.5 %copy-start.1 = (bf16[8,16,1024]{2,1,0:T(8,128)(2,1)S(1)}, bf16[8,16,1024]{2,1,0:T(8,128)(2,1)}, u32[]{:S(2)}) copy-start(bf16[8,16,1024]{2,1,0:T(8,128)(2,1)} %param.13) | copy-start | bytes 786436
  56.7 0.7 copy-start.11
  76.0 0.7 copy-start.5
  78.7 241.8 %reduce-scatter.3.cloned.1.call-start = ((), (), s32[]{:S(2)}) async-start(), calls=%async_computation.2 | async-start | bytes 6488064 | tf_op jit(solution)/shard_map/reduce_scatter | solution.py:333
  79.0 1.1 copy-start.3
  80.1 0.9 copy-start.15
  81.0 17.6 %copy-start.6 = (bf16[128,1536]{1,0:T(8,128)(2,1)S(1)}, bf16[128,1536]{1,0:T(8,128)(2,1)}, u32[]{:S(2)}) copy-start(bf16[128,1536]{1,0:T(8,128)(2,1)} %copy-done.5) | copy-start | bytes 1179652
  81.0 17.6 %copy-start.12 = (bf16[128,1024]{1,0:T(8,128)(2,1)S(1)}, bf16[128,1024]{1,0:T(8,128)(2,1)}, u32[]{:S(2)}) copy-start(bf16[128,1024]{1,0:T(8,128)(2,1)} %copy-done.11) | copy-start | bytes 786436
  98.6 2.1 copy-start.7
  98.6 1.0 copy-start.10
  103.9 309.5 %copy-start.8 = (bf16[128,1024]{1,0:T(8,128)(2,1)S(1)}, bf16[128,1024]{1,0:T(8,128)(2,1)}, u32[]{:S(2)}) copy-start(bf16[128,1024]{1,0:T(8,128)(2,1)} %copy-done.7) | copy-start | bytes 786436
  103.9 305.6 %all-reduce.4.cloned.1.call-start = ((), (), s32[]{:S(2)}) async-start(), calls=%async_computation.4 | async-start | bytes 524288 | tf_op jit(solution)/shard_map/psum | solution.py:341
Sparse Core Ops, SparseCore 0:
  78.9 114.1 reduce-scatter.4
  195.7 124.7 reduce-scatter.2
  323.4 86.0 all-reduce.3

commit v2 on v1

--- a/solution.py
+++ b/solution.py
@@ -95,17 +95,31 @@
     return jnp.where(low, both[:CELLS], both[CELLS:])
 
 
+def load_weights(layer, win_hbm, wout_hbm, win_ref, wout_ref, load_sem):
+    pairs = (
+        (win_hbm.at[layer, :, pl.ds(INNER, 2 * INNER)], win_ref.at[:, pl.ds(INNER, 2 * INNER)]),
+        (win_hbm.at[layer, :, pl.ds(0, INNER)], win_ref.at[:, pl.ds(0, INNER)]),
+        (wout_hbm.at[layer], wout_ref),
+    )
+    loads = [pltpu.make_async_copy(src, dst, load_sem.at[n]) for n, (src, dst) in enumerate(pairs)]
+    for load in loads:
+        load.start()
+    return loads
+
+
 def fwd_kernel(
-    x_ref, win_ref, wout_ref, gain_ref, bias_ref, sel_ref, coord_ref,
+    layer, x_ref, win_hbm, wout_hbm, gain_ref, bias_ref, sel_ref, coord_ref,
     y_ref, normed_ref, q_ref, kv_ref, p_ref, mixed_ref,
-    pack_ref, rw_ref, dense_ref, send_sem, recv_sem,
+    win_ref, wout_ref, pack_ref, rw_ref, dense_ref, load_sem, send_sem, recv_sem,
 ):
+    loads = load_weights(layer, win_hbm, wout_hbm, win_ref, wout_ref, load_sem)
     lat, lon = place()
     barrier = greet(lat, lon)
     x = x_ref[...].astype(F32)
     centred, rstd = norm_parts(x)
     normed = (centred * rstd * gain_ref[...]).astype(BF16)
     normed_ref[...] = normed
+    loads[0].wait()
     kv = dot(normed, win_ref[:, INNER:]).astype(BF16)
     kv_ref[0:CELLS, :] = kv
     pack_ref[...] = dot(sel_ref[...], kv).astype(BF16)
@@ -126,6 +140,7 @@
         )
         copy.start()
         copies.append(copy)
+    loads[1].wait()
     q_ref[...] = dot(normed, win_ref[:, :INNER]).astype(BF16)
     key_i = coord_ref[0:1, :]
     row_ok = (lat * ROWS + key_i >= 0) & (lat * ROWS + key_i < 64)
@@ -159,17 +174,20 @@
         p_ref[2 * pair : 2 * pair + 2] = probs.reshape(2, CELLS, KEYS)
         values = kv_ref[:, INNER + pair * 128 : INNER + pair * 128 + 128]
         mixed_ref[:, lanes] = join_heads(dot(probs.astype(BF16), values)).astype(BF16)
+    loads[2].wait()
     y_ref[...] = (x + dot(mixed_ref[...], wout_ref[...])).astype(BF16)
 
 
 def bwd_kernel(
-    up_ref, x_ref, q_ref, kv_ref, p_ref, win_ref, wout_ref, gain_ref, sel_ref, coord_ref,
+    layer, up_ref, x_ref, q_ref, kv_ref, p_ref, win_hbm, wout_hbm, gain_ref, sel_ref, coord_ref,
     down_ref, gp_ref, gain_grad_ref, bias_grad_ref,
-    part_ref, out_ref, in_ref, ds_ref, sums_ref, send_sem, recv_sem,
+    win_ref, wout_ref, part_ref, out_ref, in_ref, ds_ref, sums_ref, load_sem, send_sem, recv_sem,
 ):
+    loads = load_weights(layer, win_hbm, wout_hbm, win_ref, wout_ref, load_sem)
     lat, lon = place()
     barrier = greet(lat, lon)
     up = up_ref[...]
+    loads[2].wait()
     grad_mixed = dot(up, wout_ref[...], ((1,), (1,))).astype(BF16)
     scale = HEAD_DIM ** (-0.5)
     for pair in range(HEADS // 2):
@@ -224,7 +242,7 @@
             ones, sums_ref[...], (((1,), (1,)), ((), ())),
             precision=lax.Precision.HIGHEST, preferred_element_type=F32,
         )
-        bias_grad_ref[head] = total
+        bias_grad_ref[pl.ds(head, 1), :] = total[0:1]
         return 0
 
     lax.fori_loop(0, HEADS, collect, 0)
@@ -234,6 +252,8 @@
     part_ref[0:48, :] += in_ref[48:96, :].astype(F32)
     total = part_ref[...] + dot(sel_ref[...], in_ref[96:224, :], ((0,), (0,)))
     gp_ref[:, INNER:] = total.astype(BF16)
+    loads[0].wait()
+    loads[1].wait()
     grad_normed = dot(gp_ref[...], win_ref[...], ((1,), (1,)))
     centred, rstd = norm_parts(x_ref[...].astype(F32))
     unit = centred * rstd
@@ -248,6 +268,10 @@
     return [pl.BlockSpec(memory_space=pltpu.VMEM)] * count
 
 
+def anywhere(count):
+    return [pl.BlockSpec(memory_space=pl.ANY)] * count
+
+
 def params(collective_id):
     return pltpu.CompilerParams(
         collective_id=collective_id, has_side_effects=True, vmem_limit_bytes=48 * 1024 * 1024
@@ -258,9 +282,9 @@
     return jax.ShapeDtypeStruct(dims, dtype)
 
 
-def fwd_layer(x, win, wout, gain, bias, sel, coord):
+def fwd_layer(layer, x, win, wout, gain, bias, sel, coord):
     return pl.pallas_call(
-        fwd_kernel,
+        functools.partial(fwd_kernel, layer),
         out_shape=(
             shape((CELLS, D), BF16),
             shape((CELLS, D), BF16),
@@ -269,41 +293,338 @@
             shape((HEADS, CELLS, KEYS), F32),
             shape((CELLS, INNER), BF16),
         ),
-        in_specs=vmem(4) + [pl.BlockSpec(memory_space=pltpu.SMEM)] + vmem(2),
+        in_specs=vmem(1) + anywhere(2) + vmem(1) + [pl.BlockSpec(memory_space=pltpu.SMEM)] + vmem(2),
         out_specs=tuple(vmem(6)),
         scratch_shapes=[
+            pltpu.VMEM((D, 3 * INNER), BF16),
+            pltpu.VMEM((INNER, D), BF16),
             pltpu.VMEM((128, D), BF16),
             pltpu.VMEM((WIN, ROWS, KEYS), F32),
             pltpu.VMEM((HEADS, CELLS, KEYS), F32),
+            pltpu.SemaphoreType.DMA((3,)),
             pltpu.SemaphoreType.DMA((8,)),
             pltpu.SemaphoreType.DMA((8,)),
         ],
-        compiler_params=params(0),
+        compiler_params=params(layer),
     )(x, win, wout, gain, bias, sel, coord)
 
 
-def bwd_layer(up, x, q, kv, p, win, wout, gain, sel, coord):
+def bwd_layer(layer, up, x, q, kv, p, win, wout, gain, sel, coord):
     return pl.pallas_call(
-        bwd_kernel,
+        functools.partial(bwd_kernel, layer),
         out_shape=(
             shape((CELLS, D), BF16),
             shape((CELLS, 3 * INNER), BF16),
             shape((1, D), F32),
-            shape((HEADS, 8, 56), F32),
+            shape((HEADS, 56), F32),
         ),
-        in_specs=vmem(10),
+        in_specs=vmem(5) + anywhere(2) + vmem(3),
         out_specs=tuple(vmem(4)),
         scratch_shapes=[
+            pltpu.VMEM((D, 3 * INNER), BF16),
+            pltpu.VMEM((INNER, D), BF16),
             pltpu.VMEM((CELLS, D), F32),
             pltpu.VMEM((KEYS - CELLS, D), BF16),
             pltpu.VMEM((KEYS - CELLS, D), BF16),
             pltpu.VMEM((HEADS, CELLS, KEYS), F32),
             pltpu.VMEM((56, KEYS), F32),
+            pltpu.SemaphoreType.DMA((3,)),
             pltpu.SemaphoreType.DMA((8,)),
             pltpu.SemaphoreType.DMA((8,)),
         ],
-        compiler_params=params(1),
+        compiler_params=params(3 - layer),
     )(up, x, q, kv, p, win, wout, gain, sel, coord)
+
+
+def hop(index, step):
+    if step == 1:
+        return index + 1 - 2 * lax.rem(index, 2)
+    if step == 2:
+        return lax.rem(index + 2, 4)
+    return 3 - index
+
+
+def chip():
+    lat, lon = place()
+    x = 2 * lax.rem(lat, 2) + lax.rem(lax.div(lon, 2), 2)
+    return x, lax.div(lat, 2), lax.div(lon, 4), lax.rem(lon, 2)
+
+
+def device(x, y, z, core):
+    return (2 * y + lax.div(x, 2), 4 * z + 2 * lax.rem(x, 2) + core)
+
+
+ORDER = ((1, 3), (3, 1), (1, 3), (3, 1))
+
+
+def slot_of(core, index, x_low):
+    part = 2 * core + index // 8
+    x, y = 2 * ((index % 8) // 4) + x_low, index % 4
+    return (part, x, y) if part < 2 else (part, y, x)
+
+
+def add(a, b):
+    return (a.astype(F32) + b.astype(F32)).astype(BF16)
+
+
+class Sum:
+    def __init__(self, layer, refs, bufs, send_sem, recv_sem):
+        self.l, self.refs, self.b = layer, refs, bufs
+        self.send_sem, self.recv_sem, self.count, self.copies = send_sem, recv_sem, 0, []
+
+    def send(self, src, dst, to):
+        copy = pltpu.make_async_remote_copy(
+            src_ref=src,
+            dst_ref=dst,
+            send_sem=self.send_sem.at[self.l, self.count],
+            recv_sem=self.recv_sem.at[self.l, self.count],
+            device_id=to,
+            device_id_type=MESH,
+        )
+        copy.start()
+        self.count += 1
+        self.copies.append(copy)
+
+    def wait(self):
+        for copy in self.copies:
+            copy.wait()
+        self.copies = []
+
+    def share(self):
+        x, y, z, core = chip()
+        l, b = self.l, self.b
+        normed, packed, mixed, up = self.refs
+        to = device(x, y, z, 1 - core)
+        self.send(normed, b["nb"].at[l, pl.ds(CELLS, CELLS)], to)
+        self.send(mixed, b["mb"].at[l, pl.ds(CELLS, CELLS)], to)
+        other, mine = 1 - core, core
+        half = lambda ref, which, width: ref.at[:, pl.ds(pl.multiple_of(which * width, 128), width)]
+        self.send(half(up, other, 512), b["ub"].at[l, pl.ds(CELLS, CELLS)], to)
+        self.send(half(packed, other, 768), b["gb"].at[l, pl.ds(CELLS, CELLS)], to)
+        b["nb"][l, :CELLS] = normed[...]
+        b["mb"][l, :CELLS] = mixed[...]
+        b["ub"][l, :CELLS] = half(up, mine, 512)[...]
+        b["gb"][l, :CELLS] = half(packed, mine, 768)[...]
+
+    def product(self):
+        self.wait()
+        l, b = self.l, self.b
+        slab = b["slab"]
+
+        def step(k, _):
+            for zz in range(2):
+                z = 2 * k + zz
+                left = b["nb"][l, :, pl.ds(pl.multiple_of(z * 128, 128), 128)]
+                term = dot(left, b["gb"][l], ((0,), (0,))).astype(BF16)
+                for x_low in range(2):
+                    for rg in range(4):
+                        for cg in range(6):
+                            part, f, g = slot_of(rg // 2, (rg % 2) * 6 + cg, x_low)
+                            row = x_low * 64 + rg * 16
+                            slab[l, part, f, g, z] = term[row : row + 16, cg * 128 : cg * 128 + 128]
+            left = b["mb"][l, :, pl.ds(pl.multiple_of(k * 128, 128), 128)]
+            term = dot(left, b["ub"][l], ((0,), (0,))).astype(BF16)
+            for zz in range(2):
+                for x_low in range(2):
+                    for core in range(2):
+                        for cg in range(4):
+                            part, f, g = slot_of(core, 12 + cg, x_low)
+                            row = zz * 64 + x_low * 32 + core * 16
+                            slab[l, part, f, g, 2 * k + zz] = term[
+                                row : row + 16, cg * 128 : cg * 128 + 128
+                            ]
+            return 0
+
+        lax.fori_loop(0, 4, step, 0)
+        x, y, z, core = chip()
+        for t in range(4):
+            f = x if t < 2 else y
+            for k, step_of in enumerate((ORDER[t][0], 2)):
+                self.send(slab.at[l, t, hop(f, step_of)], b["r1"].at[l, t, k], self.peer(t, 0))
+
+    def peer(self, t, turn, second=False):
+        x, y, z, core = chip()
+        step = ORDER[t][turn]
+        if (t < 2) != second:
+            return device(hop(x, step), y, z, core)
+        return device(x, hop(y, step), z, core)
+
+    def stage(self, number):
+        self.wait()
+        l, b = self.l, self.b
+        slab = b["slab"]
+        x, y, z, core = chip()
+        if number <= 4:
+            for t in range(4):
+                f, g = (x, y) if t < 2 else (y, x)
+                last = ORDER[t][1]
+                if number == 1:
+                    slab[l, t, f] = add(slab[l, t, f], b["r1"][l, t, 0])
+                    nxt = hop(f, last)
+                    slab[l, t, nxt] = add(slab[l, t, nxt], b["r1"][l, t, 1])
+                    self.send(slab.at[l, t, nxt], b["r2"].at[l, t], self.peer(t, 1))
+                elif number == 2:
+                    slab[l, t, f] = add(slab[l, t, f], b["r2"][l, t])
+                    for k, step_of in enumerate((ORDER[t][0], 2)):
+                        self.send(
+                            slab.at[l, t, f, hop(g, step_of)], b["r3"].at[l, t, k], self.peer(t, 0, True)
+                        )
+                elif number == 3:
+                    slab[l, t, f, g] = add(slab[l, t, f, g], b["r3"][l, t, 0])
+                    nxt = hop(g, last)
+                    slab[l, t, f, nxt] = add(slab[l, t, f, nxt], b["r3"][l, t, 1])
+                    self.send(slab.at[l, t, f, nxt], b["r4"].at[l, t], self.peer(t, 1, True))
+                else:
+                    b["zs"][l, :, t] = add(slab[l, t, f, g], b["r4"][l, t])
+            if number == 4:
+                b["zr"][l, z] = b["zs"][l, z]
+                for d in range(1, 8):
+                    to = lax.rem(z + d, 8)
+                    self.send(b["zs"].at[l, to], b["zr"].at[l, z], device(x, y, to, core))
+        elif number == 5:
+            total = b["zr"][l, 0].astype(F32)
+            for k in range(1, 8):
+                total += b["zr"][l, k].astype(F32)
+            b["fin"][l] = total.astype(BF16)
+            x_high, x_low = lax.div(x, 2), lax.rem(x, 2)
+            own = 8 * core + 4 * x_high + y
+            b["ag"][l, own] = b["fin"][l, pl.ds(2 * core, 2)]
+            for d in range(1, 16):
+                to_core = 1 - core if d // 8 else core
+                to_high = 1 - x_high if (d // 4) % 2 else x_high
+                to_y = lax.rem(y + d % 4, 4)
+                self.send(
+                    b["fin"].at[l, pl.ds(2 * to_core, 2)],
+                    b["ag"].at[l, own],
+                    device(2 * to_high + x_low, to_y, z, to_core),
+                )
+        else:
+            in_out, out_out = b["in_out"], b["out_out"]
+            for slot in range(16):
+                core_of, rest = slot // 8, slot % 8
+                for half in range(2):
+                    index = half * 8 + rest
+                    tile = b["ag"][l, slot, half].astype(F32)
+                    if index < 12:
+                        row, col = 16 * (index // 6), core_of * 768 + (index % 6) * 128
+                        in_out[l, row : row + 16, col : col + 128] = tile
+                    else:
+                        col = core_of * 512 + (index - 12) * 128
+                        out_out[l, :, col : col + 128] = tile
+
+
+def sum_kernel(*args):
+    refs = [args[0:4], args[4:8]]
+    small = [args[8:10], args[10:12]]
+    in_out, out_out, gain_out, bias_out = args[12:16]
+    names = ("nb", "mb", "ub", "gb", "slab", "r1", "r2", "r3", "r4", "zs", "zr", "fin", "ag")
+    bufs = dict(zip(names, args[16:29]))
+    bufs["in_out"], bufs["out_out"] = in_out, out_out
+    vec, vec_in, vec_z, send_sem, recv_sem, vec_send, vec_recv = args[29:]
+    x, y, z, core = chip()
+    x_high, x_low = lax.div(x, 2), lax.rem(x, 2)
+    barrier = pltpu.get_barrier_semaphore()
+    peers = []
+    for d in range(1, 16):
+        to_core = 1 - core if d // 8 else core
+        to_high = 1 - x_high if (d // 4) % 2 else x_high
+        peers.append(device(2 * to_high + x_low, lax.rem(y + d % 4, 4), z, to_core))
+    for d in (1, 3):
+        peers.append(device(hop(x, d), y, z, core))
+    for d in range(1, 8):
+        peers.append(device(x, y, lax.rem(z + d, 8), core))
+    for to in peers:
+        pl.semaphore_signal(barrier, inc=1, device_id=to, device_id_type=MESH)
+    vec[...] = jnp.zeros_like(vec)
+    for l in range(LAYERS):
+        gain_grad, bias_grad = small[l]
+        for k in range(8):
+            vec[8 * l + k : 8 * l + k + 1, :] = gain_grad[:, k * 128 : k * 128 + 128]
+        vec[16 + 8 * l : 24 + 8 * l, 0:56] = bias_grad[...]
+    pl.semaphore_wait(barrier, len(peers))
+
+    def vec_send_to(n, dst, to):
+        copy = pltpu.make_async_remote_copy(
+            src_ref=vec, dst_ref=dst, send_sem=vec_send.at[n], recv_sem=vec_recv.at[n],
+            device_id=to, device_id_type=MESH,
+        )
+        copy.start()
+        return copy
+
+    vec_peers = (
+        device(x, y, z, 1 - core),
+        device(hop(x, 1), y, z, core),
+        device(hop(x, 3), y, z, core),
+        device(x, hop(y, 1), z, core),
+        device(x, hop(y, 3), z, core),
+    )
+    sums = [Sum(l, refs[l], bufs, send_sem, recv_sem) for l in range(LAYERS)]
+    sums[1].share()
+    sums[0].share()
+    copy = vec_send_to(0, vec_in.at[0], vec_peers[0])
+    sums[1].product()
+    sums[0].product()
+    for number in range(1, 7):
+        sums[1].stage(number)
+        sums[0].stage(number)
+        if number <= 5:
+            copy.wait()
+            vec[...] += vec_in[number - 1]
+            if number < 5:
+                copy = vec_send_to(number, vec_in.at[number], vec_peers[number])
+            else:
+                vec_z[z] = vec[...]
+                copies = [
+                    vec_send_to(4 + d, vec_z.at[z], device(x, y, lax.rem(z + d, 8), core))
+                    for d in range(1, 8)
+                ]
+    for copy in copies:
+        copy.wait()
+    total = vec_z[0]
+    for k in range(1, 8):
+        total += vec_z[k]
+    for l in range(LAYERS):
+        for k in range(8):
+            gain_out[l : l + 1, k * 128 : k * 128 + 128] = total[8 * l + k : 8 * l + k + 1]
+        bias_out[l] = total[16 + 8 * l : 24 + 8 * l, : WIN * WIN]
+
+
+def sum_all(layers, small):
+    tile = (16, 128)
+    return pl.pallas_call(
+        sum_kernel,
+        out_shape=(
+            shape((LAYERS, 32, 1536), F32),
+            shape((LAYERS, 16, 1024), F32),
+            shape((LAYERS, D), F32),
+            shape((LAYERS, HEADS, WIN * WIN), F32),
+        ),
+        in_specs=vmem(12),
+        out_specs=tuple(vmem(4)),
+        scratch_shapes=[
+            pltpu.VMEM((2, 2 * CELLS, D), BF16),
+            pltpu.VMEM((2, 2 * CELLS, INNER), BF16),
+            pltpu.VMEM((2, 2 * CELLS, 512), BF16),
+            pltpu.VMEM((2, 2 * CELLS, 768), BF16),
+            pltpu.VMEM((2, 4, 4, 4, 8) + tile, BF16),
+            pltpu.VMEM((2, 4, 2, 4, 8) + tile, BF16),
+            pltpu.VMEM((2, 4, 4, 8) + tile, BF16),
+            pltpu.VMEM((2, 4, 2, 8) + tile, BF16),
+            pltpu.VMEM((2, 4, 8) + tile, BF16),
+            pltpu.VMEM((2, 8, 4) + tile, BF16),
+            pltpu.VMEM((2, 8, 4) + tile, BF16),
+            pltpu.VMEM((2, 4) + tile, BF16),
+            pltpu.VMEM((2, 16, 2) + tile, BF16),
+            pltpu.VMEM((32, 128), F32),
+            pltpu.VMEM((5, 32, 128), F32),
+            pltpu.VMEM((8, 32, 128), F32),
+            pltpu.SemaphoreType.DMA((2, 50)),
+            pltpu.SemaphoreType.DMA((2, 50)),
+            pltpu.SemaphoreType.DMA((12,)),
+            pltpu.SemaphoreType.DMA((12,)),
+        ],
+        compiler_params=params(4),
+    )(*layers[0], *layers[1], *small[0], *small[1])
 
 
 def shards(inputs, input_weight, output_weight, norm_gain, position_bias, cotangent):
@@ -313,35 +634,21 @@
     stored = []
     for l in range(LAYERS):
         y, normed, q, kv, p, mixed = fwd_layer(
-            stream, input_weight[l], output_weight[l], norm_gain[l : l + 1], position_bias[l], sel, coord
+            l, stream, input_weight, output_weight, norm_gain[l : l + 1], position_bias[l], sel, coord
         )
         stored.append((stream, normed, q, kv, p, mixed))
         stream = y
     up = cotangent.reshape(CELLS, D)
-    packed_terms, output_terms = [None] * LAYERS, [None] * LAYERS
-    gain_terms, bias_terms = [None] * LAYERS, [None] * LAYERS
+    terms, small = [None] * LAYERS, [None] * LAYERS
     for l in reversed(range(LAYERS)):
         x, normed, q, kv, p, mixed = stored[l]
-        output_terms[l] = dot(mixed, up, ((0,), (0,)))
-        up, gp, gain_grad, bias_grad = bwd_layer(
-            up, x, q, kv, p, input_weight[l], output_weight[l], norm_gain[l : l + 1], sel, coord
-        )
-        packed_terms[l] = dot(normed, gp, ((0,), (0,)))
-        gain_terms[l] = gain_grad[0]
-        bias_terms[l] = bias_grad[:, 0, : WIN * WIN]
-    lon_share = (
-        lax.psum_scatter(
-            jnp.stack(packed_terms).astype(jnp.bfloat16), "lon", scatter_dimension=1, tiled=True
-        ),
-        lax.psum_scatter(
-            jnp.stack(output_terms).astype(jnp.bfloat16), "lon", scatter_dimension=1, tiled=True
-        ),
-    )
-    packed_grad, output_grad = (
-        lax.psum(lon_share[0], "lat").astype(F32),
-        lax.psum(lon_share[1], "lat").astype(F32),
-    )
-    gain_grad, bias_grad = lax.psum((jnp.stack(gain_terms), jnp.stack(bias_terms)), ("lat", "lon"))
+        down, packed, gain_grad, bias_grad = bwd_layer(
+            l, up, x, q, kv, p, input_weight, output_weight, norm_gain[l : l + 1], sel, coord
+        )
+        terms[l] = (normed, packed, mixed, up)
+        small[l] = (gain_grad, bias_grad)
+        up = down
+    packed_grad, output_grad, gain_grad, bias_grad = sum_all(terms, small)
     tile = (ROWS, COLS, D)
     return (stream.reshape(tile), up.reshape(tile), packed_grad, output_grad, gain_grad, bias_grad)
 

time: 425 us -> 131 us (0.31)
  waiting for transfers between devices: 225 us -> 0 us
  blocking collectives: 80.1 us -> 0 us
  Pallas kernels: 75.8 us -> 121 us
  between operations: 14 us -> 0.75 us
  other arithmetic: 7.98 us -> 0 us
  local copies, waits for them, and re-layouts: 14.2 us -> 9.53 us
    reduce_scatter x2 -> x0, waiting for transfers between devices: 217 us -> none  [the longest x1 128 us: shards(): lax.psum_scatter(jnp.stack(packed_terms).astype(jnp.bfloat16), 'lon', sca...]
    psum x1 -> x0, blocking collectives: 80.1 us -> none  [shards(): lax.psum((jnp.stack(gain_terms), jnp.stack(bias_terms)), ('lat', 'lon'))]
    pallas_call x4 -> x5, Pallas kernels: 75.8 us -> 121 us  [the longest x1 50.6 us: sum_all(): pl.pallas_call(sum_kernel, out_shape=(shape((LAYERS, 32, 1536), F32), sha...]
    psum x1 -> x0, waiting for transfers between devices: 8.75 us -> none  [shards(): lax.psum(lon_share[0], 'lat').astype(F32)]
    squeeze x2 -> x0, local copies, waits for them, and re-layouts: 7.57 us -> none  [the longest x1 5.86 us: shards(): input_weight[l]]
    another operation x4 -> x0, other arithmetic: 4.78 us -> none  [the longest x1 3.2 us: shards(): jnp.stack(packed_terms).astype(jnp.bfloat16)]
  transfers between devices with their start and end apart: 3 -> 0, of which waited for: 3 -> 0; matrix products, arithmetic and copies ran while one was open for 1% -> 0% of each run, Pallas kernels for 4% -> 0%
where the time goes in v2:
time: 131 us
  Pallas kernels  121 us (92%)
  local copies, waits for them, and re-layouts  9.53 us (7%)
    pallas_call x1, Pallas kernels, sum_all(): pl.pallas_call(sum_kernel, out_shape=(shape((LAYERS, 32, 1536), F32), sha...  50.6 us
    pallas_call x2, Pallas kernels, fwd_layer(): pl.pallas_call(functools.partial(fwd_kernel, layer), out_shape=(shape((CE...  37.8 us
    pallas_call x2, Pallas kernels, bwd_layer(): pl.pallas_call(functools.partial(bwd_kernel, layer), out_shape=(shape((CE...  32.2 us
    unnamed x24, local copies, waits for them, and re-layouts  8.04 us

profile of v2, /device:TPU:1, one launch (start us, length us, event | category | flops | bytes accessed | tf_op | source)
XLA Modules:
  0.0 130.8 jit_solution(15624417632178096241)
XLA Ops:
  0.6 0.8 fusion
  1.4 0.7 slice_bitcast_fusion
  2.1 0.0 copy-start
  2.1 1.6 %copy-done = bf16[2,512,1024]{2,1,0:T(8,128)(2,1)S(1)} copy-done((bf16[2,512,1024]{2,1,0:T(8,128)(2,1)S(1)}, bf16[2,512,1024]{2,1,0:T(8,128)(2,1)}, u32[]{:S(2)}) %copy-start) | copy-done | bytes 2097176
  3.7 0.0 copy-start.2
  3.7 0.9 copy-done.2
  4.7 0.0 copy-start.5
  4.7 0.8 copy-done.5
  5.4 0.0 copy-start.7
  5.4 0.7 copy-done.7
  6.1 0.0 copy-start.1
  6.1 19.9 %shard_map.127 = (bf16[128,1024]{1,0:T(8,128)(2,1)S(1)}, bf16[128,1024]{1,0:T(8,128)(2,1)S(1)}, bf16[128,512]{1,0:T(8,128)(2,1)S(1)}, bf16[352,1024]{1,0:T(8,128...) custom-call(bf16[128,1024]{1,0:T(8,128)(2,1)S(1)} %bitcast.8, bf16[2,1024,1536]{2,1,0:T(8,128)(2,1)} %win_hbm.7, ...), custom_call_target="tpu_custom_call" | custom-call | tf_op jit(solution)/shard_map/pallas_call | solution.py:286
  26.1 0.0 copy-done.1
  26.1 0.0 copy-start.4
  26.1 0.0 copy-start.8
  26.1 17.9 %shard_map.128 = (bf16[128,1024]{1,0:T(8,128)(2,1)S(1)}, bf16[128,1024]{1,0:T(8,128)(2,1)S(1)}, bf16[128,512]{1,0:T(8,128)(2,1)S(1)}, bf16[352,1024]{1,0:T(8,128...) custom-call(bf16[128,1024]{1,0:T(8,128)(2,1)S(1)} %get-tuple-element.30.x_ref, ...), custom_call_target="tpu_custom_call" | custom-call | tf_op jit(solution)/shard_map/pallas_call | solution.py:286
  44.0 0.0 copy-done.4
  44.0 0.0 copy-done.8
  44.0 0.0 copy-start.3
  44.0 0.0 copy-start.6
  44.0 16.4 %shard_map.129 = (bf16[128,1024]{1,0:T(8,128)(2,1)S(1)}, bf16[128,1536]{1,0:T(8,128)(2,1)S(1)}, f32[1,1024]{1,0:T(1,128)S(1)}, f32[8,56]{1,0:T(8,128)S(1)}) custom-call(bf16[128,1024]{1,0:T(8,128)(2,1)S(1)} %bitcast.10, bf16[128,1024]{1,0:T(8,128)(2,1)S(1)} %get-tuple-element.30.x_ref, bf16[128,512]{1,0:T(8,128)(2,1)S(1)} %get-tuple-element.32.q_ref, ...), custom_call_target="tpu_custom_call" | custom-call | tf_op jit(solution)/shard_map/pallas_call | solution.py:313
  60.5 0.0 copy-done.3
  60.5 0.0 copy-done.6
  60.5 15.8 %shard_map.130 = (bf16[128,1024]{1,0:T(8,128)(2,1)S(1)}, bf16[128,1536]{1,0:T(8,128)(2,1)S(1)}, f32[1,1024]{1,0:T(1,128)S(1)}, f32[8,56]{1,0:T(8,128)S(1)}) custom-call(bf16[128,1024]{1,0:T(8,128)(2,1)S(1)} %get-tuple-element.35.up_ref.args_3_, bf16[128,1024]{1,0:T(8,128)(2,1)S(1)} %bitcast.9, bf16[128,512]{1,0:T(8,128)(2,1)S(1)} %get-tuple-element.36.q_ref, ...), custom_call_target="tpu_custom_call" | custom-call | tf_op jit(solution)/shard_map/pallas_call | solution.py:313
  76.2 50.6 %shard_map.131 = (f32[2,32,1536]{2,1,0:T(8,128)S(1)}, f32[2,16,1024]{2,1,0:T(8,128)S(1)}, f32[2,1024]{1,0:T(2,128)S(1)}, f32[2,8,49]{2,1,0:T(8,128)S(1)}) custom-call(bf16[128,1024]{1,0:T(8,128)(2,1)S(1)} %get-tuple-element.40.args_0_, bf16[128,1536]{1,0:T(8,128)(2,1)S(1)} %get-tuple-element.41.args_1_, bf16[128,512]{1,0:T(8,128)(2,1)S(1)} %get-tuple-element.42.args_2_, ...), custom_call_target="tpu_custom_call" | custom-call | tf_op jit(solution)/shard_map/pallas_call | solution.py:594
  126.8 0.7 copy.20
  127.5 0.7 copy.21
  128.2 0.7 copy.22
  129.0 0.7 copy.23
  129.6 0.6 copy.24
  130.2 0.6 copy.25
Async XLA Ops:
  2.1 1.6 %copy-start = (bf16[2,512,1024]{2,1,0:T(8,128)(2,1)S(1)}, bf16[2,512,1024]{2,1,0:T(8,128)(2,1)}, u32[]{:S(2)}) copy-start(bf16[2,512,1024]{2,1,0:T(8,128)(2,1)} %wout_hbm.7) | copy-start | bytes 6291460
  3.7 0.9 copy-start.2
  4.7 0.8 copy-start.5
  5.4 0.7 copy-start.7
  6.1 19.9 %copy-start.1 = (bf16[2,512,1024]{2,1,0:T(8,128)(2,1)S(1)}, bf16[2,512,1024]{2,1,0:T(8,128)(2,1)}, u32[]{:S(2)}) copy-start(bf16[2,512,1024]{2,1,0:T(8,128)(2,1)} %wout_hbm.7) | copy-start | bytes 6291460
  26.1 17.9 %copy-start.4 = (bf16[8,16,1024]{2,1,0:T(8,128)(2,1)S(1)}, bf16[8,16,1024]{2,1,0:T(8,128)(2,1)}, u32[]{:S(2)}) copy-start(bf16[8,16,1024]{2,1,0:T(8,128)(2,1)} %param.13) | copy-start | bytes 786436
  26.1 17.9 %copy-start.8 = (s32[8,352]{1,0:T(8,128)S(1)}, s32[8,352]{1,0:T(8,128)}, u32[]{:S(2)}) copy-start(s32[8,352]{1,0:T(8,128)} %constant.5.clone.coord_ref) | copy-start | bytes 33796
  44.0 16.5 %copy-start.3 = (bf16[8,16,1024]{2,1,0:T(8,128)(2,1)S(1)}, bf16[8,16,1024]{2,1,0:T(8,128)(2,1)}, u32[]{:S(2)}) copy-start(bf16[8,16,1024]{2,1,0:T(8,128)(2,1)} %param.8) | copy-start | bytes 786436
  44.0 16.5 %copy-start.6 = (bf16[128,128]{1,0:T(8,128)(2,1)S(1)}, bf16[128,128]{1,0:T(8,128)(2,1)}, u32[]{:S(2)}) copy-start(bf16[128,128]{1,0:T(8,128)(2,1)} %constant.4.clone.sel_ref) | copy-start | bytes 98308

commit v3 on v1

v3 whole, which is shorter than its diff:
```python
import jax
import jax.numpy as jnp
import numpy as np
from jax import lax
from jax.experimental import pallas as pl
from jax.experimental.pallas import tpu as pltpu
from jax.sharding import PartitionSpec as P

HEADS = 8
HEAD_DIM = 64
WIN = 7
RADIUS = 3
LAYERS = 2
D = 1024
INNER = 512
ROWS, COLS = 8, 16
CELLS = ROWS * COLS
KEYS = 352
EPS = 1e-05
MESH = pl.DeviceIdType.MESH
F32, BF16 = jnp.float32, jnp.bfloat16

SEGMENTS = (
    (128, 48, -1, 0),
    (176, 48, 1, 0),
    (224, 32, 0, -1),
    (256, 32, 0, 1),
    (288, 16, -1, -1),
    (304, 16, -1, 1),
    (320, 16, 1, -1),
    (336, 16, 1, 1),
)


def geometry():
    key_coord = np.full((8, KEYS), 1000, np.int32)
    select = np.zeros((128, CELLS), np.float32)
    for i in range(ROWS):
        for j in range(COLS):
            key_coord[0, i * COLS + j], key_coord[1, i * COLS + j] = i, j
    for first, _, d_lat, d_lon in SEGMENTS:
        rows = {-1: range(5, 8), 0: range(8), 1: range(3)}[d_lat]
        cols = {-1: range(13, 16), 0: range(16), 1: range(3)}[d_lon]
        place = first
        for i in rows:
            for j in cols:
                key_coord[0, place], key_coord[1, place] = i + d_lat * ROWS, j + d_lon * COLS
                if d_lon != 0:
                    select[place - 224, i * COLS + j] = 1.0
                place += 1
    return key_coord, select


KEY_COORD, SELECT = geometry()


def place():
    return lax.axis_index("lat"), lax.axis_index("lon")


def at(lat, lon, d_lat, d_lon):
    return (lax.rem(lat + d_lat + 8, 8), lax.rem(lon + d_lon + 32, 32))


def dot(a, b, dims=((1,), (0,))):
    return lax.dot_general(a, b, (dims, ((), ())), preferred_element_type=F32)


def norm_parts(x):
    mean = jnp.mean(x, axis=-1, keepdims=True)
    centred = x - mean
    var = jnp.mean(centred * centred, axis=-1, keepdims=True)
    return centred, lax.rsqrt(var + EPS)


def split_heads(pair):
    low = lax.broadcasted_iota(jnp.int32, pair.shape, 1) < HEAD_DIM
    zero = jnp.zeros_like(pair)
    return jnp.concatenate([jnp.where(low, pair, zero), jnp.where(low, zero, pair)], axis=0)


def join_heads(both):
    low = lax.broadcasted_iota(jnp.int32, (CELLS, 2 * HEAD_DIM), 1) < HEAD_DIM
    return jnp.where(low, both[:CELLS], both[CELLS:])


def chip():
    lat, lon = place()
    x = 2 * lax.rem(lat, 2) + lax.rem(lax.div(lon, 2), 2)
    return x, lax.div(lat, 2), lax.div(lon, 4), lax.rem(lon, 2)


def device(x, y, z, core):
    return (2 * y + lax.div(x, 2), 4 * z + 2 * lax.rem(x, 2) + core)


def turn(index, step, count):
    return lax.rem(index + step, count)


def owners():
    x, y, z, core = chip()
    x_high, x_low = lax.div(x, 2), lax.rem(x, 2)
    for d in range(1, 16):
        to_core = 1 - core if d // 8 else core
        to_high = 1 - x_high if (d // 4) % 2 else x_high
        yield device(2 * to_high + x_low, turn(y, d % 4, 4), z, to_core), to_core


def across():
    x, y, z, core = chip()
    x_high, x_low = lax.div(x, 2), lax.rem(x, 2)
    for d in range(1, 16):
        to_low = 1 - x_low if d % 2 else x_low
        yield device(2 * x_high + to_low, y, turn(z, d // 2, 8), core)


def greet():
    lat, lon = place()
    x, y, z, core = chip()
    peers = [to for to, _ in owners()] + list(across()) + [device(3 - x, y, z, core)]
    peers += [at(lat, lon, d_lat, d_lon) for _, _, d_lat, d_lon in SEGMENTS if d_lon != 0]
    barrier = pltpu.get_barrier_semaphore()
    for to in peers:
        pl.semaphore_signal(barrier, inc=1, device_id=to, device_id_type=MESH)
    return barrier, len(peers)


X_FIRST = (True, False, False, True)
EARLY, LATE = (0, 2), (1, 3)


def slot_of(core, late, index, x_low):
    part = 2 * core + late
    x, y = 2 * (index // 4) + x_low, index % 4
    return (part, x, y) if X_FIRST[part] else (part, y, x)


class Sender:
    def __init__(self, send_sem, recv_sem):
        self.send_sem, self.recv_sem, self.count = send_sem, recv_sem, 0

    def __call__(self, src, dst, to):
        copy = pltpu.make_async_remote_copy(
            src_ref=src,
            dst_ref=dst,
            send_sem=self.send_sem.at[self.count],
            recv_sem=self.recv_sem.at[self.count],
            device_id=to,
            device_id_type=MESH,
        )
        copy.start()
        self.count += 1
        return copy


class Layer:
    def __init__(self, l, b, send, loads):
        self.l, self.b, self.send, self.loads = l, b, send, loads
        self.copies, self.vec_copies, self.pending = [], [], [0, 1, 2]
        self.shares, self.moves = [], {EARLY: [], LATE: [], "z": []}

    def load(self, n):
        if n in self.pending:
            self.pending.remove(n)
            self.loads[n].wait()

    def forward_start(self, x, before_send):
        b, l = self.b, self.l
        lat, lon = place()
        centred, rstd = norm_parts(x)
        normed = (centred * rstd * b["gain"][l : l + 1, :]).astype(BF16)
        b["normed"][l] = normed
        self.load(0)
        kv = dot(normed, b["win"][l, :, INNER:]).astype(BF16)
        b["kv"][l, 0:CELLS, :] = kv
        b["pack"][l] = dot(b["sel"][...], kv).astype(BF16)
        before_send()
        for first, rows, d_lat, d_lon in SEGMENTS:
            if d_lon == 0:
                source = b["kv"].at[l, pl.ds(80 if d_lat < 0 else 0, rows)]
            else:
                source = b["pack"].at[l, pl.ds(first - 224, rows)]
            to = at(lat, lon, -d_lat, -d_lon)
            self.copies.append(self.send(source, b["kv"].at[l, pl.ds(first, rows)], to))
        self.load(1)
        b["q"][l] = dot(normed, b["win"][l, :, :INNER]).astype(BF16)
        self.expand()

    def expand(self):
        b, l = self.b, self.l
        lat, lon = place()
        key_i = b["coord"][0:1, :]
        row_ok = (lat * ROWS + key_i >= 0) & (lat * ROWS + key_i < 64)
        step_lat = jnp.where(row_ok, key_i, 1000) - lax.broadcasted_iota(jnp.int32, (ROWS, KEYS), 0)
        step_lon = b["coord"][1:2, :] - lax.broadcasted_iota(jnp.int32, (COLS, KEYS), 0)
        bias, rw, dense = b["bias"], b["rw"], b["dense"]

        def step(head, _):
            for w in range(WIN):
                acc = jnp.full((ROWS, KEYS), -jnp.inf, F32)
                for u in range(WIN):
                    acc = jnp.where(step_lat == u - RADIUS, bias[l, head, u * WIN + w], acc)
                rw[w] = acc
            for i in range(ROWS):
                acc = jnp.full((COLS, KEYS), -jnp.inf, F32)
                for w in range(WIN):
                    acc = jnp.where(step_lon == w - RADIUS, rw[w, i : i + 1, :], acc)
                dense[head, i * COLS : (i + 1) * COLS, :] = acc
            return 0

        lax.fori_loop(0, HEADS, step, 0)

    def wait(self):
        for copy in self.copies:
            copy.wait()
        self.copies = []

    def forward_end(self, x):
        b, l = self.b, self.l
        self.wait()
        kv = b["kv"]
        for pair in range(HEADS // 2):
            lanes = slice(pair * 128, pair * 128 + 128)
            queries = split_heads(b["q"][l, :, lanes])
            bias = b["dense"][2 * pair : 2 * pair + 2].reshape(2 * CELLS, KEYS)
            scores = dot(queries, kv[l, :, lanes], ((1,), (1,))) * HEAD_DIM ** (-0.5) + bias
            top = jnp.max(scores, axis=-1, keepdims=True)
            weight = jnp.exp(scores - top)
            probs = weight / jnp.sum(weight, axis=-1, keepdims=True)
            b["probs"][l, 2 * pair : 2 * pair + 2] = probs.reshape(2, CELLS, KEYS)
            values = kv[l, :, INNER + pair * 128 : INNER + pair * 128 + 128]
            b["mixed"][l, :, lanes] = join_heads(dot(probs.astype(BF16), values)).astype(BF16)
        self.load(2)
        return (x + dot(b["mixed"][l], b["wout"][l])).astype(BF16)

    def mixed_grad(self, up):
        self.b["gm"][self.l] = dot(up, self.b["wout"][self.l], ((1,), (1,))).astype(BF16)

    def backward_start(self):
        b, l = self.b, self.l
        lat, lon = place()
        scale = HEAD_DIM ** (-0.5)
        kv, packed, part, out = b["kv"], b["packed"], b["part"], b["out"]
        for pair in range(HEADS // 2):
            lanes = slice(pair * 128, pair * 128 + 128)
            vlanes = slice(INNER + pair * 128, INNER + pair * 128 + 128)
            keys = kv[l, :, lanes]
            grads = split_heads(b["gm"][l, :, lanes])
            grad_probs = dot(grads, kv[l, :, vlanes], ((1,), (1,)))
            probs = b["probs"][l, 2 * pair : 2 * pair + 2].reshape(2 * CELLS, KEYS)
            delta = jnp.sum(probs * grad_probs, axis=-1, keepdims=True)
            grad_scores = probs * (grad_probs - delta)
            b["dense"][2 * pair : 2 * pair + 2] = grad_scores.reshape(2, CELLS, KEYS)
            low = grad_scores.astype(BF16)
            packed[l, :, lanes] = (join_heads(dot(low, keys)) * scale).astype(BF16)
            grad_keys = dot(low, split_heads(b["q"][l, :, lanes]), ((0,), (0,))) * scale
            grad_values = dot(probs.astype(BF16), grads, ((0,), (0,)))
            part[:, lanes] = grad_keys[:CELLS]
            part[:, vlanes] = grad_values[:CELLS]
            out[l, :, lanes] = grad_keys[CELLS:].astype(BF16)
            out[l, :, vlanes] = grad_values[CELLS:].astype(BF16)
        for first, rows, d_lat, d_lon in SEGMENTS:
            here = pl.ds(first - 128, rows)
            to = at(lat, lon, d_lat, d_lon)
            self.copies.append(self.send(out.at[l, here], b["into"].at[l, here], to))
        self.share_packed((0,))

    def collect(self):
        b, l = self.b, self.l
        key_i = jnp.broadcast_to(b["coord"][0:1, :], (COLS, KEYS))
        step_lon = b["coord"][1:2, :] - lax.broadcasted_iota(jnp.int32, (COLS, KEYS), 0)
        ones = jnp.ones((8, KEYS), F32)
        sums, vec = b["sums"], b["vec"]
        sums[...] = jnp.zeros_like(sums)
        vec[l] = jnp.zeros((16, 128), F32)

        def step(head, _):
            for u in range(WIN):
                acc = jnp.zeros((COLS, KEYS), F32)
                for i in range(ROWS):
                    acc += jnp.where(
                        key_i == i + u - RADIUS, b["dense"][head, i * COLS : (i + 1) * COLS, :], 0.0
                    )
                for w in range(WIN):
                    o = u * WIN + w
                    sums[o : o + 1, :] = jnp.sum(
                        jnp.where(step_lon == w - RADIUS, acc, 0.0), axis=0, keepdims=True
                    )
            total = lax.dot_general(
                ones, sums[...], (((1,), (1,)), ((), ())),
                precision=lax.Precision.HIGHEST, preferred_element_type=F32,
            )
            vec[l, pl.ds(8 + head, 1), 0:56] = total[0:1]
            return 0

        lax.fori_loop(0, HEADS, step, 0)

    def backward_end(self, up, x):
        b, l = self.b, self.l
        self.wait()
        part, into, packed = b["part"], b["into"], b["packed"]
        part[80:128, :] += into[l, 0:48, :].astype(F32)
        part[0:48, :] += into[l, 48:96, :].astype(F32)
        total = part[...] + dot(b["sel"][...], into[l, 96:224, :], ((0,), (0,)))
        packed[l, :, INNER:] = total.astype(BF16)
        self.share_packed((1, 2))
        grad_normed = dot(packed[l], b["win"][l], ((1,), (1,)))
        centred, rstd = norm_parts(x)
        unit = centred * rstd
        gain_grad = jnp.sum(grad_normed * unit, axis=0, keepdims=True)
        for k in range(8):
            b["vec"][l, k : k + 1, :] = gain_grad[:, k * 128 : k * 128 + 128]
        scaled = grad_normed * b["gain"][l : l + 1, :]
        mean_a = jnp.mean(scaled, axis=-1, keepdims=True)
        mean_b = jnp.mean(scaled * unit, axis=-1, keepdims=True)
        return (up.astype(F32) + rstd * (scaled - mean_a - unit * mean_b)).astype(BF16)

    def share_early(self):
        x, y, z, core = chip()
        l, b = self.l, self.b
        to, there = device(x, y, z, 1 - core), pl.ds(CELLS, CELLS)
        self.shares = [
            self.send(b["normed"].at[l], b["nb"].at[l, there], to),
            self.send(b["mixed"].at[l], b["mb"].at[l, there], to),
            self.send(self.columns(b["up"], 1 - core, 512, 0), b["ub"].at[l, there], to),
        ]
        b["nb"][l, :CELLS] = b["normed"][l]
        b["mb"][l, :CELLS] = b["mixed"][l]
        b["ub"][l, :CELLS] = self.columns(b["up"], core, 512, 0)[...]

    def columns(self, ref, core, width, start):
        return ref.at[self.l, :, pl.ds(pl.multiple_of(core * width + start, 128), width)]

    def share_packed(self, blocks):
        x, y, z, core = chip()
        l, b = self.l, self.b
        to, there = device(x, y, z, 1 - core), pl.ds(CELLS, CELLS)
        for k in blocks:
            cols = slice(256 * k, 256 * k + 256)
            source = self.columns(b["packed"], 1 - core, 256, 512 * k)
            self.shares.append(self.send(source, b["gb"].at[l, there, pl.ds(256 * k, 256)], to))
            b["gb"][l, :CELLS, cols] = self.columns(b["packed"], core, 256, 512 * k)[...]

    def product_early(self):
        l, b = self.l, self.b
        for copy in self.shares:
            copy.wait()
        self.shares = []
        slab = b["slab"]

        def step(k, _):
            for zz in range(2):
                z = 2 * k + zz
                left = b["nb"][l, :, pl.ds(pl.multiple_of(z * 128, 128), 128)]
                term = dot(left, b["gb"][l, :, 0:256], ((0,), (0,))).astype(BF16)
                for x_low in range(2):
                    for rg in range(4):
                        for cg in range(2):
                            part, f, g = slot_of(rg // 2, 0, (rg % 2) * 2 + cg, x_low)
                            row = x_low * 64 + rg * 16
                            slab[l, part, f, g, z] = term[row : row + 16, cg * 128 : cg * 128 + 128]
            left = b["mb"][l, :, pl.ds(pl.multiple_of(k * 128, 128), 128)]
            term = dot(left, b["ub"][l], ((0,), (0,))).astype(BF16)
            for zz in range(2):
                for x_low in range(2):
                    for core in range(2):
                        for cg in range(4):
                            part, f, g = slot_of(core, 0, 4 + cg, x_low)
                            row = zz * 64 + x_low * 32 + core * 16
                            slab[l, part, f, g, 2 * k + zz] = term[
                                row : row + 16, cg * 128 : cg * 128 + 128
                            ]
            return 0

        lax.fori_loop(0, 4, step, 0)
        self.start_first(EARLY)

    def product_late(self):
        l, b = self.l, self.b
        for copy in self.shares:
            copy.wait()
        self.shares = []
        slab = b["slab"]

        def step(z, _):
            left = b["nb"][l, :, pl.ds(pl.multiple_of(z * 128, 128), 128)]
            term = dot(left, b["gb"][l, :, 256:768], ((0,), (0,))).astype(BF16)
            for x_low in range(2):
                for rg in range(4):
                    for cg in range(4):
                        part, f, g = slot_of(rg // 2, 1, (rg % 2) * 4 + cg, x_low)
                        row = x_low * 64 + rg * 16
                        slab[l, part, f, g, z] = term[row : row + 16, cg * 128 : cg * 128 + 128]
            return 0

        lax.fori_loop(0, 8, step, 0)
        self.start_first(LATE)

    def start_first(self, parts):
        l, b = self.l, self.b
        x, y, z, core = chip()
        for d in (2, 1, 3):
            for t in parts:
                f = x if X_FIRST[t] else y
                to = device(turn(x, d, 4), y, z, core) if X_FIRST[t] else device(x, turn(y, d, 4), z, core)
                self.moves[parts].append(
                    self.send(b["slab"].at[l, t, turn(f, d, 4)], b["r1"].at[l, t, d - 1], to)
                )

    def arrive(self, key):
        for copy in self.moves[key]:
            copy.wait()
        self.moves[key] = []

    def first_axis(self, parts):
        self.arrive(parts)
        l, b = self.l, self.b
        slab, r1 = b["slab"], b["r1"]
        x, y, z, core = chip()
        for t in parts:
            f = x if X_FIRST[t] else y
            total = slab[l, t, f].astype(F32)
            for k in range(3):
                total += r1[l, t, k].astype(F32)
            slab[l, t, f] = total.astype(BF16)
        for d in (2, 1, 3):
            for t in parts:
                f, g = (x, y) if X_FIRST[t] else (y, x)
                to = device(x, turn(y, d, 4), z, core) if X_FIRST[t] else device(turn(x, d, 4), y, z, core)
                self.moves[parts].append(
                    self.send(slab.at[l, t, f, turn(g, d, 4)], b["r2"].at[l, t, d - 1], to)
                )

    def second_axis(self, parts):
        self.arrive(parts)
        l, b = self.l, self.b
        slab, r2 = b["slab"], b["r2"]
        x, y, z, core = chip()
        for t in parts:
            f, g = (x, y) if X_FIRST[t] else (y, x)
            total = slab[l, t, f, g].astype(F32)
            for k in range(3):
                total += r2[l, t, k].astype(F32)
            b["zs"][l, :, t] = total.astype(BF16)

    def start_third(self):
        l, b = self.l, self.b
        x, y, z, core = chip()
        b["zr"][l, z] = b["zs"][l, z]
        for d in (4, 3, 5, 2, 6, 1, 7):
            to = turn(z, d, 8)
            self.moves["z"].append(
                self.send(b["zs"].at[l, to], b["zr"].at[l, z], device(x, y, to, core))
            )

    def third_axis(self):
        self.arrive("z")
        l, b = self.l, self.b
        x, y, z, core = chip()
        total = b["zr"][l, 0].astype(F32)
        for k in range(1, 8):
            total += b["zr"][l, k].astype(F32)
        b["fin"][l] = total.astype(BF16)
        own = 8 * core + 4 * lax.div(x, 2) + y
        b["ag"][l, own] = b["fin"][l, pl.ds(2 * core, 2)]
        for to, to_core in owners():
            self.moves["z"].append(
                self.send(b["fin"].at[l, pl.ds(2 * to_core, 2)], b["ag"].at[l, own], to)
            )

    def finish(self):
        self.arrive("z")

    def small_first(self):
        l, b = self.l, self.b
        x, y, z, core = chip()
        own = 8 * core + 4 * lax.div(x, 2) + y
        b["va"][l, own] = b["vec"][l]
        for to, _ in owners():
            self.vec_copies.append(self.send(b["vec"].at[l], b["va"].at[l, own], to))

    def small_second(self):
        l, b = self.l, self.b
        x, y, z, core = chip()
        for copy in self.vec_copies:
            copy.wait()
        total = b["va"][l, 0]
        for k in range(1, 16):
            total += b["va"][l, k]
        b["vec"][l] = total
        own = 2 * z + lax.rem(x, 2)
        b["vb"][l, own] = total
        self.vec_copies = [self.send(b["vec"].at[l], b["vb"].at[l, own], to) for to in across()]

    def small_end(self):
        l, b = self.l, self.b
        for copy in self.vec_copies:
            copy.wait()
        self.vec_copies = []
        total = b["vb"][l, 0]
        for k in range(1, 16):
            total += b["vb"][l, k]
        b["small"][l] = total


TILE = (16, 128)
INPUTS = ("x_hbm", "up_hbm", "win_hbm", "wout_hbm", "gain_hbm", "bias", "sel_hbm", "coord_hbm")
OUTPUTS = ("y_out", "down_out", "ag", "small")
SCRATCH = {
    "gain": ((LAYERS, D), F32),
    "sel": ((128, CELLS), BF16),
    "coord": ((8, KEYS), jnp.int32),
    "x": ((LAYERS, CELLS, D), BF16),
    "up": ((LAYERS, CELLS, D), BF16),
    "win": ((LAYERS, D, 3 * INNER), BF16),
    "wout": ((LAYERS, INNER, D), BF16),
    "normed": ((LAYERS, CELLS, D), BF16),
    "q": ((LAYERS, CELLS, INNER), BF16),
    "kv": ((LAYERS, KEYS, D), BF16),
    "pack": ((LAYERS, 128, D), BF16),
    "probs": ((LAYERS, HEADS, CELLS, KEYS), F32),
    "mixed": ((LAYERS, CELLS, INNER), BF16),
    "rw": ((WIN, ROWS, KEYS), F32),
    "dense": ((HEADS, CELLS, KEYS), F32),
    "gm": ((LAYERS, CELLS, INNER), BF16),
    "packed": ((LAYERS, CELLS, 3 * INNER), BF16),
    "part": ((CELLS, D), F32),
    "out": ((LAYERS, KEYS - CELLS, D), BF16),
    "into": ((LAYERS, KEYS - CELLS, D), BF16),
    "sums": ((56, KEYS), F32),
    "nb": ((LAYERS, 2 * CELLS, D), BF16),
    "mb": ((LAYERS, 2 * CELLS, INNER), BF16),
    "ub": ((LAYERS, 2 * CELLS, 512), BF16),
    "gb": ((LAYERS, 2 * CELLS, 768), BF16),
    "slab": ((LAYERS, 4, 4, 4, 8) + TILE, BF16),
    "r1": ((LAYERS, 4, 3, 4, 8) + TILE, BF16),
    "r2": ((LAYERS, 4, 3, 8) + TILE, BF16),
    "zs": ((LAYERS, 8, 4) + TILE, BF16),
    "zr": ((LAYERS, 8, 4) + TILE, BF16),
    "fin": ((LAYERS, 4) + TILE, BF16),
    "y": ((2, CELLS, D), BF16),
    "vec": ((LAYERS, 16, 128), F32),
    "va": ((LAYERS, 16, 16, 128), F32),
    "vb": ((LAYERS, 16, 16, 128), F32),
}
SENDS = 2 * (16 + 6 + 24 + 7 + 15 + 30)


def kernel(*refs):
    names = INPUTS + OUTPUTS + tuple(SCRATCH)
    b = dict(zip(names, refs))
    load_sem, send_sem, recv_sem = refs[len(names) :]
    barrier, greeted = greet()
    pairs = [(b["x_hbm"], b["x"].at[0])]
    for l in range(LAYERS):
        for cols in (pl.ds(INNER, 2 * INNER), pl.ds(0, INNER)):
            pairs.append((b["win_hbm"].at[l, :, cols], b["win"].at[l, :, cols]))
        pairs.append((b["wout_hbm"].at[l], b["wout"].at[l]))
    pairs.append((b["up_hbm"], b["up"].at[1]))
    pairs += [(b[name + "_hbm"], b[name]) for name in ("gain", "sel", "coord")]
    loads = [pltpu.make_async_copy(src, dst, load_sem.at[n]) for n, (src, dst) in enumerate(pairs)]
    for n in (0, 8, 1, 9, 2, 10, 3, 7, 4, 5, 6):
        loads[n].start()
    send = Sender(send_sem, recv_sem)
    first = Layer(0, b, send, loads[1:4])
    second = Layer(1, b, send, loads[4:7])
    for n in (0, 8, 9, 10):
        loads[n].wait()
    x = b["x"][0].astype(F32)
    first.forward_start(x, lambda: pl.semaphore_wait(barrier, greeted))
    b["x"][1] = first.forward_end(x)
    x = b["x"][1].astype(F32)
    second.forward_start(x, lambda: None)
    loads[7].wait()
    second.load(2)
    second.mixed_grad(b["up"][1])
    b["y"][0] = second.forward_end(x)
    saves = [pltpu.make_async_copy(b["y"].at[0], b["y_out"], load_sem.at[11])]
    saves[0].start()
    second.share_early()
    second.backward_start()
    second.product_early()
    second.collect()
    b["up"][0] = second.backward_end(b["up"][1], b["x"][1].astype(F32))
    up = b["up"][0]
    first.mixed_grad(up)
    first.share_early()
    second.product_late()
    second.small_first()
    first.backward_start()
    first.product_early()
    second.first_axis(EARLY)
    first.collect()
    second.first_axis(LATE)
    second.small_second()
    b["y"][1] = first.backward_end(up, b["x"][0].astype(F32))
    saves.append(pltpu.make_async_copy(b["y"].at[1], b["down_out"], load_sem.at[12]))
    saves[1].start()
    first.product_late()
    first.small_first()
    second.second_axis(EARLY)
    second.second_axis(LATE)
    second.start_third()
    first.first_axis(EARLY)
    second.third_axis()
    second.small_end()
    first.first_axis(LATE)
    first.small_second()
    first.second_axis(EARLY)
    second.finish()
    first.second_axis(LATE)
    first.start_third()
    first.small_end()
    first.third_axis()
    first.finish()
    for save in saves:
        save.wait()


def lay_out(y_ref, down_ref, ag, small, y_out, down_out, in_out, out_out, gain_out, bias_out):
    y_out[...] = y_ref[...]
    down_out[...] = down_ref[...]
    for l in range(LAYERS):
        for slot in range(16):
            core_of, index = slot // 8, slot % 8
            early, late = ag[l, slot, 0].astype(F32), ag[l, slot, 1].astype(F32)
            if index < 4:
                row, col = 16 * (index // 2), 256 * core_of + 128 * (index % 2)
                in_out[l, row : row + 16, col : col + 128] = early
            else:
                col = core_of * 512 + (index - 4) * 128
                out_out[l, :, col : col + 128] = early
            row = 16 * (index // 4)
            col = 512 * (1 + (index % 4) // 2) + 256 * core_of + 128 * (index % 2)
            in_out[l, row : row + 16, col : col + 128] = late
        for k in range(8):
            gain_out[l : l + 1, k * 128 : k * 128 + 128] = small[l, k : k + 1, :]
        bias_out[l] = small[l, 8:16, : WIN * WIN]


def solution_step(inputs, input_weight, output_weight, norm_gain, position_bias, cotangent):
    whole, far = pl.BlockSpec(memory_space=pltpu.VMEM), pl.BlockSpec(memory_space=pl.ANY)
    scalars = pl.BlockSpec(memory_space=pltpu.SMEM)
    shape = jax.ShapeDtypeStruct
    results = pl.pallas_call(
        kernel,
        out_shape=(
            shape((CELLS, D), BF16),
            shape((CELLS, D), BF16),
            shape((LAYERS, 16, 2) + TILE, BF16),
            shape((LAYERS, 16, 128), F32),
        ),
        in_specs=[far] * 5 + [scalars, far, far],
        out_specs=(far, far, whole, whole),
        scratch_shapes=[pltpu.VMEM(*spec) for spec in SCRATCH.values()]
        + [
            pltpu.SemaphoreType.DMA((13,)),
            pltpu.SemaphoreType.DMA((SENDS,)),
            pltpu.SemaphoreType.DMA((SENDS,)),
        ],
        compiler_params=pltpu.CompilerParams(
            collective_id=0, has_side_effects=True, vmem_limit_bytes=60 * 1024 * 1024
        ),
    )(
        inputs.reshape(CELLS, D),
        cotangent.reshape(CELLS, D),
        input_weight,
        output_weight,
        norm_gain,
        position_bias,
        jnp.asarray(SELECT, BF16),
        jnp.asarray(KEY_COORD),
    )
    y, down, in_grad, out_grad, gain_grad, bias_grad = pl.pallas_call(
        lay_out,
        out_shape=(
            shape((CELLS, D), BF16),
            shape((CELLS, D), BF16),
            shape((LAYERS, 32, 1536), F32),
            shape((LAYERS, 16, 1024), F32),
            shape((LAYERS, D), F32),
            shape((LAYERS, HEADS, WIN * WIN), F32),
        ),
        in_specs=[whole] * 4,
        out_specs=(whole,) * 6,
    )(*results)
    tile = (ROWS, COLS, D)
    return y.reshape(tile), down.reshape(tile), in_grad, out_grad, gain_grad, bias_grad


def solution(mesh):
    return jax.shard_map(
        solution_step,
        mesh=mesh,
        in_specs=(P("lat", "lon", None), P(), P(), P(), P(), P("lat", "lon", None)),
        out_specs=(
            P("lat", "lon", None),
            P("lat", "lon", None),
            P(None, "lon", None),
            P(None, "lon", None),
            P(),
            P(),
        ),
        check_vma=False,
    )
```

time: 425 us -> 113 us (0.27); the launches traced: 421 us -> 113 us
  waiting for transfers between devices: 225 us -> 0 us
  blocking collectives: 80.1 us -> 0 us
  Pallas kernels: 75.8 us -> 112 us
  local copies, waits for them, and re-layouts: 14.2 us -> 0 us
  between operations: 14 us -> 0.64 us
  other arithmetic: 7.98 us -> 0 us
    reduce_scatter x2 -> x0, waiting for transfers between devices: 217 us -> none  [the longest x1 128 us: shards(): lax.psum_scatter(jnp.stack(packed_terms).astype(jnp.bfloat16), 'lon', sca...]
    psum x1 -> x0, blocking collectives: 80.1 us -> none  [shards(): lax.psum((jnp.stack(gain_terms), jnp.stack(bias_terms)), ('lat', 'lon'))]
    pallas_call x4 -> x2, Pallas kernels: 75.8 us -> 112 us  [the longest x1 110 us: solution_step(): pl.pallas_call(kernel, out_shape=(shape((CELLS, D), BF16), shape((CELLS,...]
    psum x1 -> x0, waiting for transfers between devices: 8.75 us -> none  [shards(): lax.psum(lon_share[0], 'lat').astype(F32)]
    squeeze x3 -> x0, local copies, waits for them, and re-layouts: 8.28 us -> none  [the longest x1 5.86 us: shards(): input_weight[l]]
    unnamed x34 -> x0, local copies, waits for them, and re-layouts: 5.08 us -> none
    another operation x4 -> x0, other arithmetic: 4.78 us -> none  [the longest x1 3.2 us: shards(): jnp.stack(packed_terms).astype(jnp.bfloat16)]
  transfers between devices with their start and end apart: 3 -> 0, of which waited for: 3 -> 0; matrix products, arithmetic and copies ran while one was open for 1% -> 0% of each run, Pallas kernels for 4% -> 0%
where the time goes in v3:
time: 113 us
  Pallas kernels  112 us (99%)
    pallas_call x1, Pallas kernels, solution_step(): pl.pallas_call(kernel, out_shape=(shape((CELLS, D), BF16), shape((CELLS,...  110 us

profile of v3, /device:TPU:1, one launch (start us, length us, event | category | flops | bytes accessed | tf_op | source)
XLA Modules:
  0.0 112.9 jit_solution(10271456489969618986)
XLA Ops:
  0.6 110.1 %shard_map.127 = (bf16[128,1024]{1,0:T(8,128)(2,1)}, bf16[128,1024]{1,0:T(8,128)(2,1)}, bf16[2,16,2,16,128]{4,3,2,1,0:T(8,128)(2,1)}, f32[2,16,128]{2,1,0:T(8,128)}) custom-call(bf16[128,1024]{1,0:T(8,128)(2,1)} %bitcast.4, bf16[128,1024]{1,0:T(8,128)(2,1)} %bitcast.5, bf16[2,1024,1536]{2,1,0:T(8,128)(2,1)} %refs_2_.1, bf16[2,512,1024]{2,1,0:T(8,128)(2,1)} %refs_3_.1, ...), custom_call_target="tpu_custom_call" | custom-call | tf_op jit(solution)/shard_map/pallas_call | solution.py:646
  110.8 2.1 %shard_map.128 = (bf16[128,1024]{1,0:T(8,128)(2,1)}, bf16[128,1024]{1,0:T(8,128)(2,1)}, f32[2,32,1536]{2,1,0:T(8,128)}, f32[2,16,1024]{2,1,0:T(8,128)}, f32[2,1024]{1,0:T(2,128)}, /*index=5*/f32[2,8,49]{2,1,0:T(8,128)}) custom-call(bf16[128,1024]{1,0:T(8,128)(2,1)} %get-tuple-element.16.y_ref, bf16[128,1024]{1,0:T(8,128)(2,1)} %get-tuple-element.17.down_ref, ...), custom_call_target="tpu_custom_call" | custom-call | tf_op jit(solution)/shard_map/pallas_call | solution.py:675

commit v4 on v3

--- a/solution.py
+++ b/solution.py
@@ -157,7 +157,8 @@
 class Layer:
     def __init__(self, l, b, send, loads):
         self.l, self.b, self.send, self.loads = l, b, send, loads
-        self.copies, self.vec_copies, self.pending = [], [], [0, 1, 2]
+        self.copies, self.vec_copies, self.pending = [], [], [0, 1, 2, 3]
+        self.late_copies = []
         self.shares, self.moves = [], {EARLY: [], LATE: [], "z": []}
 
     def load(self, n):
@@ -171,18 +172,23 @@
         centred, rstd = norm_parts(x)
         normed = (centred * rstd * b["gain"][l : l + 1, :]).astype(BF16)
         b["normed"][l] = normed
-        self.load(0)
-        kv = dot(normed, b["win"][l, :, INNER:]).astype(BF16)
-        b["kv"][l, 0:CELLS, :] = kv
-        b["pack"][l] = dot(b["sel"][...], kv).astype(BF16)
-        before_send()
-        for first, rows, d_lat, d_lon in SEGMENTS:
-            if d_lon == 0:
-                source = b["kv"].at[l, pl.ds(80 if d_lat < 0 else 0, rows)]
-            else:
-                source = b["pack"].at[l, pl.ds(first - 224, rows)]
-            to = at(lat, lon, -d_lat, -d_lon)
-            self.copies.append(self.send(source, b["kv"].at[l, pl.ds(first, rows)], to))
+        for n, which in enumerate((0, 3)):
+            self.load(which)
+            lanes = slice(INNER * n, INNER * n + INNER)
+            block = dot(normed, b["win"][l, :, INNER + INNER * n : 2 * INNER + INNER * n]).astype(BF16)
+            b["kv"][l, 0:CELLS, lanes] = block
+            b["pack"][l, :, lanes] = dot(b["sel"][...], block).astype(BF16)
+            if n == 0:
+                before_send()
+            lanes = pl.ds(INNER * n, INNER)
+            for first, rows, d_lat, d_lon in SEGMENTS:
+                if d_lon == 0:
+                    source = b["kv"].at[l, pl.ds(80 if d_lat < 0 else 0, rows), lanes]
+                else:
+                    source = b["pack"].at[l, pl.ds(first - 224, rows), lanes]
+                to = at(lat, lon, -d_lat, -d_lon)
+                move = self.send(source, b["kv"].at[l, pl.ds(first, rows), lanes], to)
+                (self.late_copies if n else self.copies).append(move)
         self.load(1)
         b["q"][l] = dot(normed, b["win"][l, :, :INNER]).astype(BF16)
         self.expand()
@@ -229,6 +235,11 @@
             weight = jnp.exp(scores - top)
             probs = weight / jnp.sum(weight, axis=-1, keepdims=True)
             b["probs"][l, 2 * pair : 2 * pair + 2] = probs.reshape(2, CELLS, KEYS)
+        self.copies, self.late_copies = self.late_copies, []
+        self.wait()
+        for pair in range(HEADS // 2):
+            lanes = slice(pair * 128, pair * 128 + 128)
+            probs = b["probs"][l, 2 * pair : 2 * pair + 2].reshape(2 * CELLS, KEYS)
             values = kv[l, :, INNER + pair * 128 : INNER + pair * 128 + 128]
             b["mixed"][l, :, lanes] = join_heads(dot(probs.astype(BF16), values)).astype(BF16)
         self.load(2)
@@ -256,14 +267,17 @@
             packed[l, :, lanes] = (join_heads(dot(low, keys)) * scale).astype(BF16)
             grad_keys = dot(low, split_heads(b["q"][l, :, lanes]), ((0,), (0,))) * scale
             grad_values = dot(probs.astype(BF16), grads, ((0,), (0,)))
-            part[:, lanes] = grad_keys[:CELLS]
-            part[:, vlanes] = grad_values[:CELLS]
-            out[l, :, lanes] = grad_keys[CELLS:].astype(BF16)
-            out[l, :, vlanes] = grad_values[CELLS:].astype(BF16)
-        for first, rows, d_lat, d_lon in SEGMENTS:
-            here = pl.ds(first - 128, rows)
-            to = at(lat, lon, d_lat, d_lon)
-            self.copies.append(self.send(out.at[l, here], b["into"].at[l, here], to))
+            half, k = pair // 2, 128 * (pair % 2)
+            part[half, :, k : k + 128] = grad_keys[:CELLS]
+            part[half, :, 256 + k : 384 + k] = grad_values[:CELLS]
+            out[l, half, :, k : k + 128] = grad_keys[CELLS:].astype(BF16)
+            out[l, half, :, 256 + k : 384 + k] = grad_values[CELLS:].astype(BF16)
+            if k:
+                for first, rows, d_lat, d_lon in SEGMENTS:
+                    here = pl.ds(first - 128, rows)
+                    to = at(lat, lon, d_lat, d_lon)
+                    move = self.send(out.at[l, half, here], b["into"].at[l, half, here], to)
+                    self.copies.append(move)
         self.share_packed((0,))
 
     def collect(self):
@@ -300,10 +314,12 @@
         b, l = self.b, self.l
         self.wait()
         part, into, packed = b["part"], b["into"], b["packed"]
-        part[80:128, :] += into[l, 0:48, :].astype(F32)
-        part[0:48, :] += into[l, 48:96, :].astype(F32)
-        total = part[...] + dot(b["sel"][...], into[l, 96:224, :], ((0,), (0,)))
-        packed[l, :, INNER:] = total.astype(BF16)
+        for half in range(2):
+            part[half, 80:128, :] += into[l, half, 0:48, :].astype(F32)
+            part[half, 0:48, :] += into[l, half, 48:96, :].astype(F32)
+            total = part[half] + dot(b["sel"][...], into[l, half, 96:224, :], ((0,), (0,)))
+            packed[l, :, INNER + 256 * half : INNER + 256 * half + 256] = total[:, :256].astype(BF16)
+            packed[l, :, 2 * INNER + 256 * half : 2 * INNER + 256 * half + 256] = total[:, 256:].astype(BF16)
         self.share_packed((1, 2))
         grad_normed = dot(packed[l], b["win"][l], ((1,), (1,)))
         centred, rstd = norm_parts(x)
@@ -525,9 +541,9 @@
     "dense": ((HEADS, CELLS, KEYS), F32),
     "gm": ((LAYERS, CELLS, INNER), BF16),
     "packed": ((LAYERS, CELLS, 3 * INNER), BF16),
-    "part": ((CELLS, D), F32),
-    "out": ((LAYERS, KEYS - CELLS, D), BF16),
-    "into": ((LAYERS, KEYS - CELLS, D), BF16),
+    "part": ((2, CELLS, 512), F32),
+    "out": ((LAYERS, 2, KEYS - CELLS, 512), BF16),
+    "into": ((LAYERS, 2, KEYS - CELLS, 512), BF16),
     "sums": ((56, KEYS), F32),
     "nb": ((LAYERS, 2 * CELLS, D), BF16),
     "mb": ((LAYERS, 2 * CELLS, INNER), BF16),
@@ -544,7 +560,7 @@
     "va": ((LAYERS, 16, 16, 128), F32),
     "vb": ((LAYERS, 16, 16, 128), F32),
 }
-SENDS = 2 * (16 + 6 + 24 + 7 + 15 + 30)
+SENDS = 2 * (32 + 6 + 24 + 7 + 15 + 30)
 
 
 def kernel(*refs):
@@ -553,22 +569,30 @@
     load_sem, send_sem, recv_sem = refs[len(names) :]
     barrier, greeted = greet()
     pairs = [(b["x_hbm"], b["x"].at[0])]
+    key_cols, value_cols, query_cols = pl.ds(INNER, INNER), pl.ds(2 * INNER, INNER), pl.ds(0, INNER)
     for l in range(LAYERS):
-        for cols in (pl.ds(INNER, 2 * INNER), pl.ds(0, INNER)):
+        for cols in (key_cols, query_cols):
             pairs.append((b["win_hbm"].at[l, :, cols], b["win"].at[l, :, cols]))
         pairs.append((b["wout_hbm"].at[l], b["wout"].at[l]))
     pairs.append((b["up_hbm"], b["up"].at[1]))
     pairs += [(b[name + "_hbm"], b[name]) for name in ("gain", "sel", "coord")]
+    pairs += [(b["win_hbm"].at[l, :, value_cols], b["win"].at[l, :, value_cols]) for l in range(LAYERS)]
     loads = [pltpu.make_async_copy(src, dst, load_sem.at[n]) for n, (src, dst) in enumerate(pairs)]
-    for n in (0, 8, 1, 9, 2, 10, 3, 7, 4, 5, 6):
+    for n in (0, 8, 1, 11, 9, 10):
         loads[n].start()
     send = Sender(send_sem, recv_sem)
-    first = Layer(0, b, send, loads[1:4])
-    second = Layer(1, b, send, loads[4:7])
+    first = Layer(0, b, send, loads[1:4] + loads[11:12])
+    second = Layer(1, b, send, loads[4:7] + loads[12:13])
     for n in (0, 8, 9, 10):
         loads[n].wait()
     x = b["x"][0].astype(F32)
-    first.forward_start(x, lambda: pl.semaphore_wait(barrier, greeted))
+
+    def begin():
+        for n in (2, 3, 4, 12, 5, 7, 6):
+            loads[n].start()
+        pl.semaphore_wait(barrier, greeted)
+
+    first.forward_start(x, begin)
     b["x"][1] = first.forward_end(x)
     x = b["x"][1].astype(F32)
     second.forward_start(x, lambda: None)
@@ -576,7 +600,7 @@
     second.load(2)
     second.mixed_grad(b["up"][1])
     b["y"][0] = second.forward_end(x)
-    saves = [pltpu.make_async_copy(b["y"].at[0], b["y_out"], load_sem.at[11])]
+    saves = [pltpu.make_async_copy(b["y"].at[0], b["y_out"], load_sem.at[13])]
     saves[0].start()
     second.share_early()
     second.backward_start()
@@ -586,16 +610,16 @@
     up = b["up"][0]
     first.mixed_grad(up)
     first.share_early()
+    second.small_first()
+    second.first_axis(EARLY)
+    first.backward_start()
     second.product_late()
-    second.small_first()
-    first.backward_start()
     first.product_early()
-    second.first_axis(EARLY)
     first.collect()
     second.first_axis(LATE)
     second.small_second()
     b["y"][1] = first.backward_end(up, b["x"][0].astype(F32))
-    saves.append(pltpu.make_async_copy(b["y"].at[1], b["down_out"], load_sem.at[12]))
+    saves.append(pltpu.make_async_copy(b["y"].at[1], b["down_out"], load_sem.at[14]))
     saves[1].start()
     first.product_late()
     first.small_first()
@@ -655,7 +679,7 @@
         out_specs=(far, far, whole, whole),
         scratch_shapes=[pltpu.VMEM(*spec) for spec in SCRATCH.values()]
         + [
-            pltpu.SemaphoreType.DMA((13,)),
+            pltpu.SemaphoreType.DMA((15,)),
             pltpu.SemaphoreType.DMA((SENDS,)),
             pltpu.SemaphoreType.DMA((SENDS,)),
         ],

time: 113 us -> 108 us (0.956)
  Pallas kernels: 112 us -> 107 us
    pallas_call x1, Pallas kernels: 110 us -> 105 us  [solution_step(): pl.pallas_call(kernel, out_shape=(shape((CELLS, D), BF16), shape((CELLS,...]
where the time goes in v4:
time: 108 us; the launch traced here: 107 us
  Pallas kernels  107 us (99%)
    pallas_call x1, Pallas kernels, solution_step(): pl.pallas_call(kernel, out_shape=(shape((CELLS, D), BF16), shape((CELLS,...  105 us

profile of v4, /device:TPU:1, one launch (start us, length us, event | category | flops | bytes accessed | tf_op | source)
XLA Modules:
  0.0 107.3 jit_solution(1973096554452066115)
XLA Ops:
  0.6 104.6 %shard_map.127 = (bf16[128,1024]{1,0:T(8,128)(2,1)}, bf16[128,1024]{1,0:T(8,128)(2,1)}, bf16[2,16,2,16,128]{4,3,2,1,0:T(8,128)(2,1)}, f32[2,16,128]{2,1,0:T(8,128)}) custom-call(bf16[128,1024]{1,0:T(8,128)(2,1)} %bitcast.4, bf16[128,1024]{1,0:T(8,128)(2,1)} %bitcast.5, bf16[2,1024,1536]{2,1,0:T(8,128)(2,1)} %refs_2_.1, bf16[2,512,1024]{2,1,0:T(8,128)(2,1)} %refs_3_.1, ...), custom_call_target="tpu_custom_call" | custom-call | tf_op jit(solution)/shard_map/pallas_call | solution.py:670
  105.2 2.1 %shard_map.128 = (bf16[128,1024]{1,0:T(8,128)(2,1)}, bf16[128,1024]{1,0:T(8,128)(2,1)}, f32[2,32,1536]{2,1,0:T(8,128)}, f32[2,16,1024]{2,1,0:T(8,128)}, f32[2,1024]{1,0:T(2,128)}, /*index=5*/f32[2,8,49]{2,1,0:T(8,128)}) custom-call(bf16[128,1024]{1,0:T(8,128)(2,1)} %get-tuple-element.16.y_ref, bf16[128,1024]{1,0:T(8,128)(2,1)} %get-tuple-element.17.down_ref, ...), custom_call_target="tpu_custom_call" | custom-call | tf_op jit(solution)/shard_map/pallas_call | solution.py:699

commit v5 on v4

--- a/solution.py
+++ b/solution.py
@@ -23,12 +23,12 @@
 SEGMENTS = (
     (128, 48, -1, 0),
     (176, 48, 1, 0),
-    (224, 32, 0, -1),
-    (256, 32, 0, 1),
     (288, 16, -1, -1),
     (304, 16, -1, 1),
     (320, 16, 1, -1),
     (336, 16, 1, 1),
+    (224, 32, 0, -1),
+    (256, 32, 0, 1),
 )
 
 
@@ -312,14 +312,16 @@
 
     def backward_end(self, up, x):
         b, l = self.b, self.l
-        self.wait()
         part, into, packed = b["part"], b["into"], b["packed"]
         for half in range(2):
+            for copy in self.copies[8 * half : 8 * half + 8]:
+                copy.wait()
             part[half, 80:128, :] += into[l, half, 0:48, :].astype(F32)
             part[half, 0:48, :] += into[l, half, 48:96, :].astype(F32)
             total = part[half] + dot(b["sel"][...], into[l, half, 96:224, :], ((0,), (0,)))
             packed[l, :, INNER + 256 * half : INNER + 256 * half + 256] = total[:, :256].astype(BF16)
             packed[l, :, 2 * INNER + 256 * half : 2 * INNER + 256 * half + 256] = total[:, 256:].astype(BF16)
+        self.copies = []
         self.share_packed((1, 2))
         grad_normed = dot(packed[l], b["win"][l], ((1,), (1,)))
         centred, rstd = norm_parts(x)

time: 108 us -> 108 us (level)
  no operation moved by 1% of the time
where the time goes in v5:
time: 108 us
  Pallas kernels  107 us (99%)
    pallas_call x1, Pallas kernels, solution_step(): pl.pallas_call(kernel, out_shape=(shape((CELLS, D), BF16), shape((CELLS,...  105 us

profile of v5, /device:TPU:1, one launch (start us, length us, event | category | flops | bytes accessed | tf_op | source)
XLA Modules:
  0.0 107.5 jit_solution(8509340190212698514)
XLA Ops:
  0.6 104.8 %shard_map.127 = (bf16[128,1024]{1,0:T(8,128)(2,1)}, bf16[128,1024]{1,0:T(8,128)(2,1)}, bf16[2,16,2,16,128]{4,3,2,1,0:T(8,128)(2,1)}, f32[2,16,128]{2,1,0:T(8,128)}) custom-call(bf16[128,1024]{1,0:T(8,128)(2,1)} %bitcast.4, bf16[128,1024]{1,0:T(8,128)(2,1)} %bitcast.5, bf16[2,1024,1536]{2,1,0:T(8,128)(2,1)} %refs_2_.1, bf16[2,512,1024]{2,1,0:T(8,128)(2,1)} %refs_3_.1, ...), custom_call_target="tpu_custom_call" | custom-call | tf_op jit(solution)/shard_map/pallas_call | solution.py:672
  105.4 2.1 %shard_map.128 = (bf16[128,1024]{1,0:T(8,128)(2,1)}, bf16[128,1024]{1,0:T(8,128)(2,1)}, f32[2,32,1536]{2,1,0:T(8,128)}, f32[2,16,1024]{2,1,0:T(8,128)}, f32[2,1024]{1,0:T(2,128)}, /*index=5*/f32[2,8,49]{2,1,0:T(8,128)}) custom-call(bf16[128,1024]{1,0:T(8,128)(2,1)} %get-tuple-element.16.y_ref, bf16[128,1024]{1,0:T(8,128)(2,1)} %get-tuple-element.17.down_ref, ...), custom_call_target="tpu_custom_call" | custom-call | tf_op jit(solution)/shard_map/pallas_call | solution.py:701
